TPU v7x, 512 devices: a whole 4x4x16 slice. The times are simulated.
512 devices in a mesh: batch: 16 (over x, z_hi, core), head: 32 (over z_lo, y).
Axes of the slice: x: 4, y: 4, z: 16 (z_hi: 2, z_lo: 8; z = z_hi * 8 + z_lo), core: 2. Of those that a mesh axis runs over, the one named last changes fastest.
Arguments:
- student_patches: bfloat16 [64, 256, 256], P('batch')
- teacher_patches: bfloat16 [64, 256, 256], P('batch')
- mask_index: int32 [64, 128], P('batch'), may hold values from 0 to 255, as said below
- weight: bfloat16 [256, 65536], P(None, 'head')
Outputs:
- grad_rows: float32 [64, 128, 256], P('batch')
- grad_weight: float32 [256, 65536], P('batch', 'head')
- loss: float32 [], replicated
Inputs may be any that keep to these rules, and one draw needn't show every extreme that they name: `mask_index`: the 128 positions of one crop are distinct.
All inputs are finite; a program needn't handle non-finite values.
Results may differ from a plain program's by a relative error of at most 0.003.
Values sent between devices are 32-bit elements; how exact they have to be, the bound alone decides.
No kernel may reach another device: no remote copies, remote signals or barrier semaphores. Data moves between devices by JAX's collectives and lax.ppermute only.
A program may use at most 64 MiB of HBM per device.

v0:
```python
import jax
import jax.numpy as jnp
from jax import lax
from jax.sharding import PartitionSpec as P

TEACHER_TEMP = 0.07
STUDENT_TEMP = 0.1
EPSILON = 1e-06
HIGH = lax.Precision.HIGHEST


def unit_rows(values):
    floats = values.astype(jnp.float32)
    inverse = lax.rsqrt(jnp.sum(floats * floats, axis=-1, keepdims=True) + EPSILON)
    return (floats * inverse, inverse)


def contract_rows(left, right):
    return lax.dot_general(
        left, right, (((0,), (0,)), ((), ())), preferred_element_type=jnp.float32
    )


def per_device(student_patches, teacher_patches, mask_index, weight):
    view_count, masked_count = mask_index.shape
    feature_dim = weight.shape[0]
    gather_index = mask_index[:, :, None]
    student_rows = jnp.take_along_axis(student_patches, gather_index, axis=1).reshape(
        -1, feature_dim
    )
    teacher_rows = jnp.take_along_axis(teacher_patches, gather_index, axis=1).reshape(
        -1, feature_dim
    )
    student_unit, student_inv = unit_rows(student_rows)
    teacher_unit, teacher_inv = unit_rows(teacher_rows)
    student_norm = student_unit.astype(jnp.bfloat16)
    teacher_norm = teacher_unit.astype(jnp.bfloat16)
    wfloat = weight.astype(jnp.float32)
    weight_inv = lax.rsqrt(jnp.sum(wfloat * wfloat, axis=0, keepdims=True) + EPSILON)
    weight_unit = wfloat * weight_inv
    weight_norm = weight_unit.astype(jnp.bfloat16)
    teacher_exp = jnp.exp(
        jnp.dot(teacher_norm, weight_norm, preferred_element_type=jnp.float32) / TEACHER_TEMP
    )
    row_scale = jnp.ones((teacher_exp.shape[0],), jnp.float32)
    col_scale = jnp.ones((teacher_exp.shape[1],), jnp.float32)
    for sweep in range(3):
        col_total = lax.psum(jnp.dot(row_scale, teacher_exp, precision=HIGH), "batch")
        col_scale = 1.0 / col_total
        if sweep < 2:
            row_total = lax.psum(jnp.dot(teacher_exp, col_scale, precision=HIGH), "head")
            row_scale = 1.0 / row_total
    student_logits = jnp.dot(student_norm, weight_norm, preferred_element_type=jnp.float32)
    student_exp = jnp.exp(student_logits / STUDENT_TEMP)
    partition_part = jnp.sum(student_exp, axis=1)
    row_part = jnp.dot(teacher_exp, col_scale, precision=HIGH)
    row_total = lax.psum(row_part, "head")
    row_scale = 1.0 / row_total
    targets = row_scale[:, None] * teacher_exp * col_scale[None, :]
    weighted_part = jnp.sum(targets * student_logits, axis=1)
    partition, weighted = lax.psum((partition_part, weighted_part), "head")
    row_loss = jnp.log(partition) - weighted / STUDENT_TEMP
    total_rows = row_loss.shape[0] * lax.axis_size("batch")
    loss = lax.psum(jnp.sum(row_loss), "batch") / total_rows
    grad_logits = ((student_exp / partition[:, None] - targets) / STUDENT_TEMP).astype(jnp.bfloat16)
    grad_local = lax.dot_general(
        grad_logits, weight_norm, (((1,), (1,)), ((), ())), preferred_element_type=jnp.float32
    )
    grad_student = lax.psum(grad_local, "head")
    inner = jnp.sum(student_unit * grad_student, axis=1, keepdims=True)
    grad_rows = (student_inv * (grad_student - student_unit * inner)).reshape(
        view_count, masked_count, feature_dim
    )
    share = feature_dim // lax.axis_size("batch")
    offset = lax.axis_index("batch") * share
    grad_unit = lax.psum(contract_rows(student_norm, grad_logits), "batch")
    col_inner = jnp.sum(weight_unit * grad_unit, axis=0, keepdims=True)
    grad_full = weight_inv * (grad_unit - weight_unit * col_inner)
    grad_weight = lax.dynamic_slice_in_dim(grad_full, offset, share, 0)
    return (grad_rows, grad_weight, loss)


def solution(mesh):
    in_specs = (P("batch", None, None), P("batch", None, None), P("batch", None), P(None, "head"))
    out_specs = (P("batch", None, None), P("batch", "head"), P())
    return jax.shard_map(
        per_device, mesh=mesh, in_specs=in_specs, out_specs=out_specs, check_vma=False
    )
```

profile of v0, /device:TPU:120, one launch (start us, length us, event | category | flops | bytes accessed | tf_op | source)
XLA Modules:
  0.0 1509.3 jit_solution(325576755089128837)
XLA Ops:
  7.2 0.8 or_bitcast_fusion
  8.0 0.7 and_bitcast_fusion
  8.7 3.2 gather_fusion
  11.9 7.0 gather_fusion.1
  19.8 0.8 multiply_exponential_fusion
  20.6 1.9 copy-done.1
  22.6 2.1 fusion.11
  24.6 75.2 %psum.78 = f32[2048]{0:T(1024)S(1)} all-reduce(f32[2048]{0:T(1024)S(1)} %bitcast.70), channel_id=1, replica_groups=mesh['batch'=16,'head'=32] {'batch'}, use_global_device_ids=true, to_apply=%region_5.0 | all-reduce | flops 2048 | bytes 16384 | tf_op jit(solution)/shard_map/psum | solution.py:48
  99.9 5.8 fusion.14
  105.6 69.4 %psum.79 = f32[512]{0:T(512)S(1)} all-reduce(f32[512]{0:T(512)S(1)} %bitcast.71), channel_id=1, replica_groups=mesh['batch'=16,'head'=32] {'head'}, use_global_device_ids=true, to_apply=%region_6.0 | all-reduce | flops 512 | bytes 4096 | tf_op jit(solution)/shard_map/psum | solution.py:51
  175.0 4.3 fusion.15
  179.3 62.8 %psum.80 = f32[2048]{0:T(1024)S(1)} all-reduce(f32[2048]{0:T(1024)S(1)} %bitcast.67), channel_id=1, replica_groups=mesh['batch'=16,'head'=32] {'batch'}, use_global_device_ids=true, to_apply=%region_7.0 | all-reduce | flops 2048 | bytes 16384 | tf_op jit(solution)/shard_map/psum | solution.py:48
  242.1 5.8 fusion.16
  247.9 104.2 %psum.81 = f32[512]{0:T(512)S(1)} all-reduce(f32[512]{0:T(512)S(1)} %bitcast.73), channel_id=1, replica_groups=mesh['batch'=16,'head'=32] {'head'}, use_global_device_ids=true, to_apply=%region_8.0 | all-reduce | flops 512 | bytes 4096 | tf_op jit(solution)/shard_map/psum | solution.py:51
  352.0 4.3 fusion.17
  356.3 62.8 %psum.82 = f32[2048]{0:T(1024)S(1)} all-reduce(f32[2048]{0:T(1024)S(1)} %bitcast.69), channel_id=1, replica_groups=mesh['batch'=16,'head'=32] {'batch'}, use_global_device_ids=true, to_apply=%region_9.0 | all-reduce | flops 2048 | bytes 16384 | tf_op jit(solution)/shard_map/psum | solution.py:48
  419.1 5.8 fusion.18
  424.8 112.7 %psum.83 = f32[512]{0:T(512)S(1)} all-reduce(f32[512]{0:T(512)S(1)} %bitcast.75), channel_id=1, replica_groups=mesh['batch'=16,'head'=32] {'head'}, use_global_device_ids=true, to_apply=%region_10.0 | all-reduce | flops 512 | bytes 4096 | tf_op jit(solution)/shard_map/psum | solution.py:57
  537.8 5.5 multiply_reduce_fusion
  543.3 114.8 %all-reduce = (f32[512]{0:T(512)S(1)}, f32[512]{0:T(512)S(1)}) all-reduce(f32[512]{0:T(512)S(1)} %get-tuple-element.5, f32[512]{0:T(512)S(1)} %get-tuple-element.4), channel_id=1, replica_groups=mesh['batch'=16,'head'=32] {'head'}, use_global_device_ids=true, to_apply=%region_3.0 | all-reduce | flops 1024 | bytes 8192 | tf_op jit(solution)/shard_map/psum | solution.py:61
  658.1 4.2 multiply_convert_fusion
  662.3 1.3 copy-done.3
  663.6 1.6 fusion.3
  665.2 3.7 fusion.19
  668.9 0.6 subtract_reduce_fusion
  669.5 62.6 %psum.87 = f32[]{:T(128)} all-reduce(f32[]{:T(128)} %subtract_reduce_fusion), channel_id=1, replica_groups=mesh['batch'=16,'head'=32] {'batch'}, use_global_device_ids=true, to_apply=%region_18.0 | all-reduce | flops 1 | bytes 8 | tf_op jit(solution)/shard_map/psum | solution.py:64
  732.8 384.3 %all-reduce.4.cloned.1.call-done = f32[512,256]{1,0:T(8,128)} async-done(((f32[512,256]{1,0:T(8,128)}), f32[512,256]{1,0:T(8,128)}) %all-reduce.4.cloned.1.call-update) | async-done | bytes 524304 | tf_op jit(solution)/shard_map/psum | solution.py:69
  1117.2 1.3 multiply_reduce_fusion.2
  1118.5 2.1 subtract_multiply_fusion
  1120.6 377.2 %all-reduce.6.cloned.1.call-done = f32[256,2048]{1,0:T(8,128)} async-done(((f32[256,2048]{1,0:T(8,128)}), f32[256,2048]{1,0:T(8,128)}) %all-reduce.6.cloned.1.call-update) | async-done | bytes 2097168 | tf_op jit(solution)/shard_map/psum | solution.py:76
  1497.8 1.9 multiply_reduce_fusion.1
  1499.8 1.6 fusion.10
  (24 shorter events, 1.3 us)
Async XLA Ops:
  7.2 1.6 copy-start
  7.2 12.3 copy-start.2
  7.2 1110.0 %all-reduce.4.cloned.1.call-start = ((), (), s32[]{:S(2)}) async-start(), calls=%async_computation | async-start | bytes 1048576 | tf_op jit(solution)/shard_map/psum | solution.py:69
  20.6 1.9 copy-start.1
  662.3 1.3 copy-start.3
  665.2 832.6 %all-reduce.6.cloned.1.call-start = ((), (), s32[]{:S(2)}) async-start(), calls=%async_computation.1 | async-start | bytes 4194304 | tf_op jit(solution)/shard_map/psum | solution.py:76
Sparse Core Ops, SparseCore 0:
  665.3 451.8 all-reduce.3
  1120.4 377.4 all-reduce.5
where the time goes:
time: 1510 us
  waiting for transfers between devices  762 us (50%)
  blocking collectives  664 us (44%)
  matrix products  39.4 us (3%)
  between operations  16 us (1%)
    psum x1, waiting for transfers between devices, per_device(): grad_student = lax.psum(grad_local, 'head')  384 us
    psum x1, waiting for transfers between devices, per_device(): grad_unit = lax.psum(contract_rows(student_norm, grad_logits), 'batch')  377 us
    psum x3, blocking collectives, per_device(): lax.psum(jnp.dot(row_scale, teacher_exp, precision=HIGH), 'batch')  201 us
    psum x2, blocking collectives, per_device(): lax.psum(jnp.dot(teacher_exp, col_scale, precision=HIGH), 'head')  174 us
    psum x1, blocking collectives, per_device(): partition, weighted = lax.psum((partition_part, weighted_part), 'head')  115 us
    psum x1, blocking collectives, per_device(): row_total = lax.psum(row_part, 'head')  113 us
    psum x1, blocking collectives, per_device(): loss = lax.psum(jnp.sum(row_loss), 'batch') / total_rows  62.6 us
  transfers between devices with their start and end apart: 2, of which 2 were waited for; matrix products, arithmetic and copies ran while one was open for 1% of the time, Pallas kernels for 0%

commit v1 on v0

v1 whole, which is shorter than its diff:
```python
import jax
import jax.numpy as jnp
from jax import lax
from jax.sharding import PartitionSpec as P

TEACHER_TEMP = 0.07
STUDENT_TEMP = 0.1
EPSILON = 1e-06


def unit_rows(values):
    inverse = lax.rsqrt(jnp.sum(values * values, axis=-1, keepdims=True) + EPSILON)
    return (values * inverse, inverse)


def contract_rows(left, right):
    return lax.dot_general(
        left, right, (((0,), (0,)), ((), ())), preferred_element_type=jnp.float32
    )


def pick_rows(patches, onehot):
    rows = lax.dot_general(
        onehot, patches, (((2,), (1,)), ((0,), (0,))), preferred_element_type=jnp.float32
    )
    return rows.reshape(-1, patches.shape[-1])


def share_all(block, axis, groups=None, count=None):
    copies = jnp.broadcast_to(block[None], (count,) + block.shape)
    return lax.all_to_all(copies, axis, 0, 0, axis_index_groups=groups)


def sum_small(vector, axis):
    count = lax.axis_size(axis)
    return jnp.sum(share_all(vector.reshape(-1, 128), axis, None, count), axis=0).reshape(
        vector.shape
    )


def scatter_sum(blocks, axis, groups):
    return jnp.sum(lax.all_to_all(blocks, axis, 0, 0, axis_index_groups=groups), axis=0)


def per_device(student_patches, teacher_patches, mask_index, weight):
    view_count, masked_count = mask_index.shape
    feature_dim, columns = weight.shape
    batch_index = lax.axis_index("batch")
    head_index = lax.axis_index("head")
    x_groups = [[4 * x + rest for x in range(4)] for rest in range(4)]
    y_groups = [[4 * z + y for y in range(4)] for z in range(8)]
    z_groups = [[4 * z + y for z in range(8)] for y in range(4)]
    core = batch_index % 2
    z_high = (batch_index // 2) % 2

    patch = lax.broadcasted_iota(jnp.int32, mask_index.shape + (student_patches.shape[1],), 2)
    onehot = (mask_index[:, :, None] == patch).astype(jnp.bfloat16)
    student_unit, student_inv = unit_rows(pick_rows(student_patches, onehot))
    teacher_unit, _ = unit_rows(pick_rows(teacher_patches, onehot))
    student_norm = student_unit.astype(jnp.bfloat16)
    teacher_norm = teacher_unit.astype(jnp.bfloat16)
    wfloat = weight.astype(jnp.float32)
    weight_inv = lax.rsqrt(jnp.sum(wfloat * wfloat, axis=0, keepdims=True) + EPSILON)
    weight_unit = wfloat * weight_inv
    weight_norm = weight_unit.astype(jnp.bfloat16)
    teacher_exp = jnp.exp(
        jnp.dot(teacher_norm, weight_norm, preferred_element_type=jnp.float32) / TEACHER_TEMP
    )
    col_scale = 1.0 / sum_small(jnp.sum(teacher_exp, axis=0), "batch")
    for _ in range(2):
        row_scale = 1.0 / sum_small(jnp.sum(teacher_exp * col_scale[None, :], axis=1), "head")
        col_scale = 1.0 / sum_small(jnp.sum(teacher_exp * row_scale[:, None], axis=0), "batch")
    student_logits = jnp.dot(student_norm, weight_norm, preferred_element_type=jnp.float32)
    student_exp = jnp.exp(student_logits / STUDENT_TEMP)
    partition_part = jnp.sum(student_exp, axis=1)
    scaled = teacher_exp * col_scale[None, :]
    row_part = jnp.sum(scaled, axis=1)
    weighted_part = jnp.sum(scaled * student_logits, axis=1)
    row_total, partition, weighted = sum_small(
        jnp.stack([row_part, partition_part, weighted_part]), "head"
    )
    row_scale = 1.0 / row_total
    row_loss = jnp.log(partition) - row_scale * weighted / STUDENT_TEMP
    total_rows = row_loss.shape[0] * lax.axis_size("batch")
    loss_part = jnp.broadcast_to(jnp.sum(row_loss), (1, 128))
    loss = sum_small(loss_part, "batch")[0, 0] / total_rows

    targets = row_scale[:, None] * scaled
    grad_logits = ((student_exp / partition[:, None] - targets) / STUDENT_TEMP).astype(jnp.bfloat16)

    grad_unit = contract_rows(student_norm, grad_logits)
    col_inner = jnp.sum(weight_unit * grad_unit, axis=0, keepdims=True)
    grad_full = weight_inv * (grad_unit - weight_unit * col_inner)
    parts = grad_full.reshape(4, 2, 2, feature_dim // 16, columns)
    keep = lax.dynamic_index_in_dim(parts, core, 2, keepdims=False)
    send = lax.dynamic_index_in_dim(parts, 1 - core, 2, keepdims=False)
    parts = keep + lax.ppermute(send, "batch", [(i, i ^ 1) for i in range(16)])
    parts = scatter_sum(parts, "batch", x_groups)
    keep = lax.dynamic_index_in_dim(parts, z_high, 0, keepdims=False)
    send = lax.dynamic_index_in_dim(parts, 1 - z_high, 0, keepdims=False)
    grad_weight = keep + lax.ppermute(send, "batch", [(i, i ^ 2) for i in range(16)])

    grad_local = lax.dot_general(
        grad_logits, weight_norm, (((1,), (1,)), ((), ())), preferred_element_type=jnp.float32
    )
    total = grad_local.shape[0]
    piece = scatter_sum(grad_local.reshape(4, total // 4, feature_dim), "head", y_groups)
    piece = scatter_sum(piece.reshape(8, total // 32, feature_dim), "head", z_groups)
    first = (head_index % 4) * (total // 4) + (head_index // 4) * (total // 32)
    unit_piece = lax.dynamic_slice_in_dim(student_unit, first, total // 32, 0)
    inv_piece = lax.dynamic_slice_in_dim(student_inv, first, total // 32, 0)
    inner = jnp.sum(unit_piece * piece, axis=1, keepdims=True)
    piece = inv_piece * (piece - unit_piece * inner)
    piece = share_all(piece, "head", z_groups, 8).reshape(total // 4, feature_dim)
    grad_rows = share_all(piece, "head", y_groups, 4).reshape(
        view_count, masked_count, feature_dim
    )
    return (grad_rows, grad_weight, loss)


def solution(mesh):
    in_specs = (P("batch", None, None), P("batch", None, None), P("batch", None), P(None, "head"))
    out_specs = (P("batch", None, None), P("batch", "head"), P())
    return jax.shard_map(
        per_device, mesh=mesh, in_specs=in_specs, out_specs=out_specs, check_vma=False
    )
```

time: 1510 us -> 278 us (0.18)
  the two profiles are of different devices: /device:TPU:120 before, /device:TPU:40 now
where the time goes in v1:
time: 278 us; the launch traced here: 277 us
  blocking collectives  105 us (38%)
  waiting for transfers between devices  87.2 us (31%)
  starting transfers between devices  39.1 us (14%)
  other arithmetic  22.3 us (8%)
  matrix products  14.7 us (5%)
  local copies, waits for them, and re-layouts  6.51 us (2%)
    all_to_all x4, blocking collectives, share_all(): return lax.all_to_all(copies, axis, 0, 0, axis_index_groups=groups)  90.3 us
    all_to_all x5, waiting for transfers between devices, share_all(): return lax.all_to_all(copies, axis, 0, 0, axis_index_groups=groups)  63.6 us
    all_to_all x5, starting transfers between devices, share_all(): return lax.all_to_all(copies, axis, 0, 0, axis_index_groups=groups)  22.2 us
    all_to_all x1, blocking collectives, scatter_sum(): lax.all_to_all(blocks, axis, 0, 0, axis_index_groups=groups)  14.9 us
    ppermute x1, waiting for transfers between devices, per_device(): lax.ppermute(send, 'batch', [(i, i ^ 2) for i in range(16)])  12.8 us
    all_to_all x2, starting transfers between devices, scatter_sum(): lax.all_to_all(blocks, axis, 0, 0, axis_index_groups=groups)  12.4 us
    all_to_all x2, waiting for transfers between devices, scatter_sum(): lax.all_to_all(blocks, axis, 0, 0, axis_index_groups=groups)  10.9 us
  transfers between devices with their start and end apart: 9, of which 8 were waited for; matrix products, arithmetic and copies ran while one was open for 3% of the time, Pallas kernels for 0%

profile of v1, /device:TPU:40, one launch (start us, length us, event | category | flops | bytes accessed | tf_op | source)
XLA Modules:
  0.0 277.1 jit_solution(3279188952772560738)
XLA Ops:
  3.4 4.1 %fusion.27 = (f32[2048]{0:T(1024)S(1)}, f32[512,2048]{1,0:T(8,128)}) fusion(bf16[512,256]{1,0:T(8,128)(2,1)S(1)} %fusion.13, bf16[256,2048]{1,0:T(8,128)(2,1)} %param.7, f32[2048]{0:T(1024)S(1)} %add_rsqrt_fusion), kind=kOutput, calls=%fused_computation.59 | convolution fusion | flops 540538880 | bytes 5521408 | tf_op jit(solution)/shard_map/dot_general | solution.py:67
  7.5 36.2 %all_to_all.60 = f32[16,16,128]{2,1,0:T(8,128)S(1)} all-to-all(f32[16,16,128]{2,1,0:T(8,128)S(1)} %broadcast_in_dim.31), channel_id=1, replica_groups=mesh['batch'=16,'head'=32] {'batch'}, dimensions={0} | all-to-all | bytes 262144 | tf_op jit(solution)/shard_map/all_to_all | solution.py:31
  43.7 2.6 multiply_reduce_fusion.4
  46.3 16.2 %all_to_all.61 = f32[32,4,128]{2,1,0:T(4,128)S(1)} all-to-all(f32[32,4,128]{2,1,0:T(4,128)S(1)} %broadcast_in_dim.33), channel_id=1, replica_groups=mesh['batch'=16,'head'=32] {'head'}, dimensions={0} | all-to-all | bytes 131072 | tf_op jit(solution)/shard_map/all_to_all | solution.py:31
  62.6 2.5 multiply_reduce_fusion.3
  65.2 22.2 %all_to_all.62 = f32[16,16,128]{2,1,0:T(8,128)S(1)} all-to-all(f32[16,16,128]{2,1,0:T(8,128)S(1)} %broadcast_in_dim.35), channel_id=1, replica_groups=mesh['batch'=16,'head'=32] {'batch'}, dimensions={0} | all-to-all | bytes 262144 | tf_op jit(solution)/shard_map/all_to_all | solution.py:31
  87.4 2.6 multiply_reduce_fusion.2
  90.0 15.7 %all_to_all.63 = f32[32,4,128]{2,1,0:T(4,128)S(1)} all-to-all(f32[32,4,128]{2,1,0:T(4,128)S(1)} %broadcast_in_dim.74), channel_id=1, replica_groups=mesh['batch'=16,'head'=32] {'head'}, dimensions={0} | all-to-all | bytes 131072 | tf_op jit(solution)/shard_map/all_to_all | solution.py:31
  105.8 2.5 multiply_reduce_fusion.1
  109.0 3.5 %all-to-all-start.4 = ((f32[16,16,128]{2,1,0:T(8,128)}), f32[16,16,128]{2,1,0:T(8,128)S(1)}, u32[]{:S(2)}, u32[]{:S(2)}) async-start(f32[16,16,128]{2,1,0:T(8,128)} %broadcast_in_dim.76), calls=%async_computation.4 | async-start | bytes 262144 | tf_op jit(solution)/shard_map/all_to_all | solution.py:31
  113.1 19.0 %all-to-all-done.4 = f32[16,16,128]{2,1,0:T(8,128)S(1)} async-done(((f32[16,16,128]{2,1,0:T(8,128)}), f32[16,16,128]{2,1,0:T(8,128)S(1)}, u32[]{:S(2)}, u32[]{:S(2)}) %all-to-all-start.4) | async-done | bytes 131104 | tf_op jit(solution)/shard_map/all_to_all | solution.py:31
  132.2 5.5 %multiply_reduce_fusion.5 = (f32[512]{0:T(512)S(1)}, f32[512]{0:T(512)S(1)}, f32[512]{0:T(512)S(1)}, f32[512,2048]{1,0:T(8,128)}) fusion(f32[512,2048]{1,0:T(8,128)} %get-tuple-element.16, f32[2048]{0:T(1024)S(1)} %divide_bitcast_fusion, bf16[256,2048]{1,0:T(8,128)(2,1)S(1)} %copy-done.1, f32[2048]{0:T(1024)S(1)} %add_rsqrt_fusion, ...), kind=kOutput, calls=%fused_computation.9 | convolution fusion | flops 544864768 | bytes 9984000 | tf_op jit(solution)/shard_map/dot_general | solution.py:73
  138.4 5.3 %all-to-all-start.5 = ((f32[32,12,128]{2,1,0:T(8,128)}), f32[32,12,128]{2,1,0:T(8,128)S(1)}, u32[]{:S(2)}, u32[]{:S(2)}) async-start(f32[32,12,128]{2,1,0:T(8,128)} %broadcast_in_dim.78), calls=%async_computation.5 | async-start | bytes 524288 | tf_op jit(solution)/shard_map/all_to_all | solution.py:31
  143.7 16.3 %all-to-all-done.5 = f32[32,12,128]{2,1,0:T(8,128)S(1)} async-done(((f32[32,12,128]{2,1,0:T(8,128)}), f32[32,12,128]{2,1,0:T(8,128)S(1)}, u32[]{:S(2)}, u32[]{:S(2)}) %all-to-all-start.5) | async-done | bytes 196640 | tf_op jit(solution)/shard_map/all_to_all | solution.py:31
  160.7 4.2 %multiply_convert_fusion = bf16[512,2048]{1,0:T(8,128)(2,1)S(1)} fusion(f32[512,2048]{1,0:T(8,128)} %get-tuple-element.17, f32[512,2048]{1,0:T(8,128)} %get-tuple-element.16, f32[512]{0:T(512)S(1)} %get-tuple-element.7, f32[512]{0:T(512)S(1)} %get-tuple-element.8, f32[2048]{0:T(1024)S(1)} %divide_bitcast_fusion), kind=kLoop, calls=%fused_computation | loop fusion | flops 7340032 | bytes 10498048 | tf_op jit(solution)/shard_map/convert_element_type | solution.py:89
  164.9 2.1 fusion.4
  167.0 1.6 fusion.8
  168.6 5.7 %all-to-all-start.6 = ((f32[4,128,256]{2,1,0:T(8,128)}), f32[4,128,256]{2,1,0:T(8,128)S(1)}, u32[]{:S(2)}, u32[]{:S(2)}) async-start(f32[4,128,256]{2,1,0:T(8,128)} %bitcast.21), calls=%async_computation.6 | async-start | bytes 1048576 | tf_op jit(solution)/shard_map/all_to_all | solution.py:42
  174.2 1.9 fusion.6
  177.6 1.9 collective-permute-start
  181.6 6.8 %all-to-all-start.7 = ((f32[8,16,256]{2,1,0:T(8,128)}), f32[8,16,256]{2,1,0:T(8,128)S(1)}, u32[]{:S(2)}, u32[]{:S(2)}) async-start(f32[8,16,256]{2,1,0:T(8,128)} %bitcast.22), calls=%async_computation.7 | async-start | bytes 262144 | tf_op jit(solution)/shard_map/all_to_all | solution.py:42
  188.4 9.5 %all-to-all-done.7 = f32[8,16,256]{2,1,0:T(8,128)S(1)} async-done(((f32[8,16,256]{2,1,0:T(8,128)}), f32[8,16,256]{2,1,0:T(8,128)S(1)}, u32[]{:S(2)}, u32[]{:S(2)}) %all-to-all-start.7) | async-done | bytes 131104 | tf_op jit(solution)/shard_map/all_to_all | solution.py:42
  199.2 3.5 %all-to-all-start.11 = ((f32[16,1,128]{2,1,0:T(1,128)}), f32[16,1,128]{2,1,0:T(1,128)S(1)}, u32[]{:S(2)}, u32[]{:S(2)}) async-start(f32[16,1,128]{2,1,0:T(1,128)} %broadcast_in_dim_broadcast_in_dim_broadcast_in_dim.3), calls=%async_computation.11 | async-start | bytes 16384 | tf_op jit(solution)/shard_map/all_to_all | solution.py:31
  202.9 14.4 %all-to-all-done.11 = f32[16,1,128]{2,1,0:T(1,128)S(1)} async-done(((f32[16,1,128]{2,1,0:T(1,128)}), f32[16,1,128]{2,1,0:T(1,128)S(1)}, u32[]{:S(2)}, u32[]{:S(2)}) %all-to-all-start.11) | async-done | bytes 8224 | tf_op jit(solution)/shard_map/all_to_all | solution.py:31
  218.0 5.1 %all-to-all-start.8 = ((f32[8,16,256]{2,1,0:T(8,128)}), f32[8,16,256]{2,1,0:T(8,128)S(1)}, u32[]{:S(2)}, u32[]{:S(2)}) async-start(f32[8,16,256]{2,1,0:T(8,128)} %broadcast_in_dim.79), calls=%async_computation.8 | async-start | bytes 262144 | tf_op jit(solution)/shard_map/all_to_all | solution.py:31
  223.0 1.7 bitcast_add_fusion
  224.7 9.8 %all-to-all-done.8 = f32[8,16,256]{2,1,0:T(8,128)S(1)} async-done(((f32[8,16,256]{2,1,0:T(8,128)}), f32[8,16,256]{2,1,0:T(8,128)S(1)}, u32[]{:S(2)}, u32[]{:S(2)}) %all-to-all-start.8) | async-done | bytes 131104 | tf_op jit(solution)/shard_map/all_to_all | solution.py:31
  234.5 14.9 %all_to_all.64 = f32[4,2,16,2048]{3,2,1,0:T(8,128)S(1)} all-to-all(f32[4,2,16,2048]{3,2,1,0:T(8,128)S(1)} %bitcast_add_fusion), channel_id=1, replica_groups={{0,128,256,384},{32,160,288,416},{64,192,320,448},{96,224,352,480},{1,1..., dimensions={0} | all-to-all | bytes 2097152 | tf_op jit(solution)/shard_map/all_to_all | solution.py:42
  250.2 4.9 %all-to-all-start.9 = ((f32[4,128,256]{2,1,0:T(8,128)}), f32[4,128,256]{2,1,0:T(8,128)S(1)}, u32[]{:S(2)}, u32[]{:S(2)}) async-start(f32[4,128,256]{2,1,0:T(8,128)} %broadcast_in_dim.81), calls=%async_computation.9 | async-start | bytes 1048576 | tf_op jit(solution)/shard_map/all_to_all | solution.py:31
  255.2 2.5 collective-permute-start.1
  257.8 4.0 %all-to-all-done.9 = f32[4,128,256]{2,1,0:T(8,128)S(1)} async-done(((f32[4,128,256]{2,1,0:T(8,128)}), f32[4,128,256]{2,1,0:T(8,128)S(1)}, u32[]{:S(2)}, u32[]{:S(2)}) %all-to-all-start.9) | async-done | bytes 524320 | tf_op jit(solution)/shard_map/all_to_all | solution.py:31
  261.8 12.8 %collective-permute-done.1 = f32[16,2048]{1,0:T(8,128)S(1)} collective-permute-done((f32[16,2048]{1,0:T(8,128)S(1)}, f32[16,2048]{1,0:T(8,128)S(1)}, u32[]{:S(2)}, u32[]{:S(2)}) %collective-permute-start.1) | collective-permute-done | bytes 131104 | tf_op jit(solution)/shard_map/ppermute | solution.py:101
  (54 shorter events, 13.5 us)
Async XLA Ops:
  0.6 1.5 copy-start
  87.4 25.1 %copy-start.3 = (bf16[4,256,256]{2,1,0:T(8,128)(2,1)S(1)}, bf16[4,256,256]{2,1,0:T(8,128)(2,1)}, u32[]{:S(2)}) copy-start(bf16[4,256,256]{2,1,0:T(8,128)(2,1)} %param.4) | copy-start | bytes 1572868
  87.4 25.1 %copy-start.4 = (s32[4,128]{1,0:T(4,128)S(1)}, s32[4,128]{1,0:T(4,128)}, u32[]{:S(2)}) copy-start(s32[4,128]{1,0:T(4,128)} %param.6) | copy-start | bytes 6148
  90.0 42.1 %copy-start.1 = (bf16[256,2048]{1,0:T(8,128)(2,1)S(1)}, bf16[256,2048]{1,0:T(8,128)(2,1)}, u32[]{:S(2)}) copy-start(bf16[256,2048]{1,0:T(8,128)(2,1)} %param.7) | copy-start | bytes 3145732
  109.0 23.1 %all-to-all-start.4 = ((f32[16,16,128]{2,1,0:T(8,128)}), f32[16,16,128]{2,1,0:T(8,128)S(1)}, u32[]{:S(2)}, u32[]{:S(2)}) async-start(f32[16,16,128]{2,1,0:T(8,128)} %broadcast_in_dim.76), calls=%async_computation.4 | async-start | bytes 262144 | tf_op jit(solution)/shard_map/all_to_all | solution.py:31
  138.4 21.6 %all-to-all-start.5 = ((f32[32,12,128]{2,1,0:T(8,128)}), f32[32,12,128]{2,1,0:T(8,128)S(1)}, u32[]{:S(2)}, u32[]{:S(2)}) async-start(f32[32,12,128]{2,1,0:T(8,128)} %broadcast_in_dim.78), calls=%async_computation.5 | async-start | bytes 524288 | tf_op jit(solution)/shard_map/all_to_all | solution.py:31
  168.6 12.3 %all-to-all-start.6 = ((f32[4,128,256]{2,1,0:T(8,128)}), f32[4,128,256]{2,1,0:T(8,128)S(1)}, u32[]{:S(2)}, u32[]{:S(2)}) async-start(f32[4,128,256]{2,1,0:T(8,128)} %bitcast.21), calls=%async_computation.6 | async-start | bytes 1048576 | tf_op jit(solution)/shard_map/all_to_all | solution.py:42
  176.2 1.4 copy-start.2
  177.6 45.4 %collective-permute-start = (f32[4,2,16,2048]{3,2,1,0:T(8,128)S(1)}, f32[4,2,16,2048]{3,2,1,0:T(8,128)}, u32[]{:S(2)}, u32[]{:S(2)}) collective-permute-start(f32[4,2,16,2048]{3,2,1,0:T(8,128)S(1)} %dynamic-slice_bitcast_fusion), channel_id=1, source_target_pairs={{0,32},{32,0},{64,96},{96,64},{128,160},{160,128},{192,224},{224,1... | collective-permute-start | bytes 3145736 | tf_op jit(solution)/shard_map/ppermute | solution.py:97
  181.6 16.4 %all-to-all-start.7 = ((f32[8,16,256]{2,1,0:T(8,128)}), f32[8,16,256]{2,1,0:T(8,128)S(1)}, u32[]{:S(2)}, u32[]{:S(2)}) async-start(f32[8,16,256]{2,1,0:T(8,128)} %bitcast.22), calls=%async_computation.7 | async-start | bytes 262144 | tf_op jit(solution)/shard_map/all_to_all | solution.py:42
  199.2 18.1 %all-to-all-start.11 = ((f32[16,1,128]{2,1,0:T(1,128)}), f32[16,1,128]{2,1,0:T(1,128)S(1)}, u32[]{:S(2)}, u32[]{:S(2)}) async-start(f32[16,1,128]{2,1,0:T(1,128)} %broadcast_in_dim_broadcast_in_dim_broadcast_in_dim.3), calls=%async_computation.11 | async-start | bytes 16384 | tf_op jit(solution)/shard_map/all_to_all | solution.py:31
  218.0 16.6 %all-to-all-start.8 = ((f32[8,16,256]{2,1,0:T(8,128)}), f32[8,16,256]{2,1,0:T(8,128)S(1)}, u32[]{:S(2)}, u32[]{:S(2)}) async-start(f32[8,16,256]{2,1,0:T(8,128)} %broadcast_in_dim.79), calls=%async_computation.8 | async-start | bytes 262144 | tf_op jit(solution)/shard_map/all_to_all | solution.py:31
  250.2 11.5 %all-to-all-start.9 = ((f32[4,128,256]{2,1,0:T(8,128)}), f32[4,128,256]{2,1,0:T(8,128)S(1)}, u32[]{:S(2)}, u32[]{:S(2)}) async-start(f32[4,128,256]{2,1,0:T(8,128)} %broadcast_in_dim.81), calls=%async_computation.9 | async-start | bytes 1048576 | tf_op jit(solution)/shard_map/all_to_all | solution.py:31
  255.2 19.3 %collective-permute-start.1 = (f32[16,2048]{1,0:T(8,128)S(1)}, f32[16,2048]{1,0:T(8,128)S(1)}, u32[]{:S(2)}, u32[]{:S(2)}) collective-permute-start(f32[16,2048]{1,0:T(8,128)S(1)} %dynamic-slice_bitcast_fusion.1), channel_id=1, source_target_pairs={{0,64},{32,96},{64,0},{96,32},{128,192},{160,224},{192,128},{224,1... | collective-permute-start | bytes 393224 | tf_op jit(solution)/shard_map/ppermute | solution.py:101

commit v2 on v0

v2 whole, which is shorter than its diff:
```python
import functools

import jax
import jax.numpy as jnp
from jax import lax
from jax.experimental import pallas as pl
from jax.experimental.pallas import tpu as pltpu
from jax.sharding import PartitionSpec as P

TEACHER_TEMP = 0.07
STUDENT_TEMP = 0.1
EPSILON = 1e-06
LANES = 128
F32 = jnp.float32
BF16 = jnp.bfloat16
MIB = 1 << 20


def kernel_call(body, out_shape, scratch=(), limit=40, scalars=0):
    whole = pl.BlockSpec(memory_space=pltpu.VMEM)

    def call(*args):
        specs = [pl.BlockSpec(memory_space=pltpu.SMEM)] * scalars
        specs += [whole] * (len(args) - scalars)
        return pl.pallas_call(
            body,
            out_shape=out_shape,
            in_specs=specs,
            out_specs=jax.tree.map(lambda _: whole, out_shape),
            scratch_shapes=list(scratch),
            compiler_params=pltpu.CompilerParams(vmem_limit_bytes=limit * MIB),
        )(*args)

    return call


def shape(dims, dtype=F32):
    return jax.ShapeDtypeStruct(dims, dtype)


def picked_unit(patches, positions):
    patch = lax.broadcasted_iota(jnp.int32, (patches.shape[0], positions.shape[1]), 0)
    onehot = (patch == positions).astype(F32).astype(BF16)
    rows = lax.dot_general(
        onehot, patches, (((0,), (0,)), ((), ())), preferred_element_type=F32
    )
    inverse = lax.rsqrt(jnp.sum(rows * rows, axis=1, keepdims=True) + EPSILON)
    return rows * inverse, inverse


def lane_tiles(row, count):
    return jnp.concatenate(
        [jnp.broadcast_to(row[i : i + 1, :], (8, LANES)) for i in range(count)], axis=1
    )


def column(row):
    return jnp.transpose(jnp.broadcast_to(row, (LANES, LANES)))


def fold(block):
    tiles = [block[:, i : i + LANES] for i in range(0, block.shape[1], LANES)]
    while len(tiles) > 1:
        tiles = [a + b for a, b in zip(tiles[::2], tiles[1::2])]
    return tiles[0]


def row_sums(partial):
    total = lax.dot_general(
        jnp.ones((8, LANES), F32),
        partial,
        (((1,), (1,)), ((), ())),
        precision=lax.Precision.HIGHEST,
        preferred_element_type=F32,
    )
    return jnp.concatenate(
        [total[0:1, i : i + LANES] for i in range(0, partial.shape[0], LANES)], axis=0
    )


def col_tiles(total):
    return jnp.concatenate(
        [total[:, i : i + LANES] for i in range(0, total.shape[1], LANES)], axis=0
    )


def split_dot(values, right):
    high = values.astype(BF16)
    low = (values - high.astype(F32)).astype(BF16)
    return jnp.dot(high, right, preferred_element_type=F32) + jnp.dot(
        low, right, preferred_element_type=F32
    )


def teacher_kernel(index_ref, patches_ref, weight_ref, exp_ref, norm_ref, inv_ref, msg_ref):
    wide = weight_ref[...].astype(F32)
    inverse = lax.rsqrt(jnp.sum(wide * wide, axis=0, keepdims=True) + EPSILON)
    inv_ref[...] = inverse
    norm_ref[...] = (wide * inverse).astype(BF16)
    total = jnp.zeros((1, weight_ref.shape[1]), F32)
    for view in range(patches_ref.shape[0]):
        unit, _ = picked_unit(patches_ref[view], index_ref[view : view + 1, :])
        logits = jnp.dot(unit.astype(BF16), norm_ref[...], preferred_element_type=F32)
        block = jnp.exp(logits * (1.0 / TEACHER_TEMP))
        exp_ref[view * LANES : (view + 1) * LANES, :] = block
        total += jnp.sum(block, axis=0, keepdims=True)
    msg_ref[...] = jnp.broadcast_to(col_tiles(total)[None], msg_ref.shape)


def student_kernel(
    index_ref, patches_ref, norm_ref,
    unit_ref, inv_ref, flip_ref, back_ref, logits_ref, exp_ref, part_ref, pull_ref,
    tail,
):
    back_ref[...] = jnp.transpose(norm_ref[...])
    for view in range(patches_ref.shape[0]):
        rows = slice(view * LANES, (view + 1) * LANES)
        unit, inverse = picked_unit(patches_ref[view], index_ref[view : view + 1, :])
        unit_ref[rows, :] = unit
        inv_ref[rows, :] = jnp.broadcast_to(inverse, (LANES, LANES))
        narrow = unit.astype(BF16)
        flip_ref[:, rows] = jnp.transpose(narrow)
        logits = jnp.dot(narrow, norm_ref[...], preferred_element_type=F32)
        block = jnp.exp(logits * (1.0 / STUDENT_TEMP))
        logits_ref[rows, :] = logits
        exp_ref[rows, :] = block
        tail[rows, :] = fold(block)
        pull_ref[rows, :] = split_dot(block, back_ref[...])
    part_ref[...] = row_sums(tail[...])


def row_kernel(has_extra, *refs):
    if has_extra:
        cols_ref, exp_ref, extra_ref, msg_ref, tail = refs
    else:
        cols_ref, exp_ref, msg_ref, tail = refs
    scale = lane_tiles(1.0 / jnp.sum(cols_ref[...], axis=0), cols_ref.shape[1])

    def step(i, carry):
        start = pl.multiple_of(i * 8, 8)
        tail[pl.ds(start, 8), :] = fold(exp_ref[pl.ds(start, 8), :] * scale)
        return carry

    lax.fori_loop(0, exp_ref.shape[0] // 8, step, 0, unroll=8)
    out = row_sums(tail[...])
    if has_extra:
        out = jnp.concatenate([out, extra_ref[...]], axis=0)
    msg_ref[...] = jnp.broadcast_to(out[None], msg_ref.shape)


def col_kernel(has_extra, rows_ref, exp_ref, *refs):
    if has_extra:
        msg_ref, extra_ref, scale_ref = refs
    else:
        msg_ref, scale_ref = refs
    total = jnp.sum(rows_ref[...], axis=0)
    if has_extra:
        extra_ref[...] = total[4:8, :]
    scale = 1.0 / total[0:4, :]
    for j in range(4):
        scale_ref[j * LANES : (j + 1) * LANES, :] = column(scale[j : j + 1, :])
    count = exp_ref.shape[1] // LANES

    def step(i, sums):
        start = pl.multiple_of(i * 8, 8)
        factor = scale_ref[pl.ds(start, 8), :]
        return tuple(
            sums[k] + exp_ref[pl.ds(start, 8), k * LANES : (k + 1) * LANES] * factor
            for k in range(count)
        )

    sums = lax.fori_loop(
        0, exp_ref.shape[0] // 8, step, (jnp.zeros((8, LANES), F32),) * count, unroll=8
    )
    total = jnp.concatenate([jnp.sum(s, axis=0, keepdims=True) for s in sums], axis=0)
    msg_ref[...] = jnp.broadcast_to(total[None], msg_ref.shape)


def last_row_kernel(cols_ref, exp_ref, logits_ref, msg_ref, scale_ref, tail, weighted):
    small = 1.0 / jnp.sum(cols_ref[...], axis=0)
    scale = lane_tiles(small, cols_ref.shape[1])
    scale_ref[...] = scale

    def step(i, carry):
        start = pl.multiple_of(i * 8, 8)
        scaled = exp_ref[pl.ds(start, 8), :] * scale
        tail[pl.ds(start, 8), :] = fold(scaled)
        weighted[pl.ds(start, 8), :] = fold(scaled * logits_ref[pl.ds(start, 8), :])
        return carry

    lax.fori_loop(0, exp_ref.shape[0] // 8, step, 0, unroll=4)
    out = jnp.concatenate([row_sums(tail[...]), row_sums(weighted[...])], axis=0)
    msg_ref[...] = jnp.broadcast_to(out[None], msg_ref.shape)


def pull_kernel(scale_ref, exp_ref, back_ref, pull_ref):
    for j in range(4):
        rows = slice(j * LANES, (j + 1) * LANES)
        pull_ref[j] = split_dot(exp_ref[rows, :] * scale_ref[0:1, :], back_ref[...])


def grad_kernel(
    core_ref, rows_ref, partition_ref, scale_ref, exp_ref, student_ref, flip_ref, weight_ref,
    inv_ref, keep_ref, send_ref, loss_ref, row_scale_ref, factor, softener, logits,
):
    total = jnp.sum(rows_ref[...], axis=0)
    partition = partition_ref[...]
    scale = 1.0 / total[0:4, :]
    row_scale_ref[...] = scale
    losses = jnp.log(partition) - scale * total[4:8, :] * (1.0 / STUDENT_TEMP)
    loss = jnp.sum(jnp.sum(losses, axis=1, keepdims=True), axis=0, keepdims=True)
    loss_ref[...] = jnp.broadcast_to(loss[None], loss_ref.shape)
    softener_rows = 1.0 / partition
    for j in range(4):
        rows = slice(j * LANES, (j + 1) * LANES)
        factor[rows, :] = column(scale[j : j + 1, :])
        softener[rows, :] = column(softener_rows[j : j + 1, :])
    width = logits.shape[1]
    core = core_ref[0]
    wide = (LANES, width)
    for block in range(exp_ref.shape[1] // width):
        cols = slice(block * width, (block + 1) * width)
        for j in range(4):
            rows = slice(j * LANES, (j + 1) * LANES)
            soft = jnp.concatenate([softener[rows, :]] * (width // LANES), axis=1)
            hard = jnp.concatenate([factor[rows, :]] * (width // LANES), axis=1)
            targets = hard * (exp_ref[rows, cols] * scale_ref[0:1, cols])
            logits[rows, :] = (
                (student_ref[rows, cols] * soft - targets) * (1.0 / STUDENT_TEMP)
            ).astype(BF16)
        unit = jnp.dot(flip_ref[...], logits[...], preferred_element_type=F32)
        inverse = inv_ref[:, cols]
        weight_unit = weight_ref[:, cols].astype(F32) * inverse
        inner = jnp.sum(weight_unit * unit, axis=0, keepdims=True)
        full = (inverse * (unit - weight_unit * inner)).reshape(4, 2, 2, 16, width)
        first, second = full[:, :, 0], full[:, :, 1]
        keep_ref[:, :, :, cols] = jnp.where(core == 0, first, second)
        send_ref[:, :, :, cols] = jnp.where(core == 0, second, first)


def exchange(blocks, axis, groups=None):
    return lax.all_to_all(blocks, axis, 0, 0, axis_index_groups=groups)


def share(block, axis, groups, count):
    return exchange(jnp.broadcast_to(block[None], (count,) + block.shape), axis, groups)


def tie(*values):
    return lax.optimization_barrier(values)


def pick(blocks, index):
    return lax.dynamic_index_in_dim(blocks, index, 0, keepdims=False)


def per_device(student_patches, teacher_patches, mask_index, weight):
    view_count, masked_count = mask_index.shape
    feature_dim, columns = weight.shape
    total = view_count * masked_count
    share_rows = feature_dim // 16
    batch_index = lax.axis_index("batch")
    head_index = lax.axis_index("head")
    x_index = batch_index // 4
    z_high = (batch_index // 2) % 2
    core = batch_index % 2
    y_index = head_index % 4
    y_groups = [[4 * z + y for y in range(4)] for z in range(8)]
    z_groups = [[4 * z + y for z in range(8)] for y in range(4)]
    col_msg = shape((16, columns // LANES, LANES))
    row_msg = shape((32, total // LANES, LANES))
    row_msg_two = shape((32, 2 * total // LANES, LANES))
    tail = pltpu.VMEM((total, LANES), F32)

    teacher_exp, weight_norm, weight_inv, cols = kernel_call(
        teacher_kernel,
        (shape((total, columns)), shape((feature_dim, columns), BF16), shape((1, columns)), col_msg),
    )(mask_index, teacher_patches, weight)
    student_patches, cols = tie(student_patches, cols)
    cols = exchange(cols, "batch")

    unit, inverse, flip, back, logits, student_exp, partition_part, student_pull = kernel_call(
        student_kernel,
        (
            shape((total, feature_dim)),
            shape((total, LANES)),
            shape((feature_dim, total), BF16),
            shape((columns, feature_dim), BF16),
            shape((total, columns)),
            shape((total, columns)),
            shape((total // LANES, LANES)),
            shape((total, feature_dim)),
        ),
        [tail],
    )(mask_index, student_patches, weight_norm)

    rows = kernel_call(functools.partial(row_kernel, True), row_msg_two, [tail])(
        cols, teacher_exp, partition_part
    )
    rows = exchange(rows, "head")
    student_piece = lax.psum_scatter(
        student_pull.reshape(4, total // 4, feature_dim), "head", axis_index_groups=y_groups
    )
    cols, partition = kernel_call(
        functools.partial(col_kernel, True), (col_msg, shape((total // LANES, LANES))), [tail]
    )(rows, teacher_exp)
    cols = exchange(cols, "batch")
    cols, student_piece = tie(cols, student_piece)
    student_piece = lax.psum_scatter(
        student_piece.reshape(8, total // 32, feature_dim), "head", axis_index_groups=z_groups
    )
    rows = kernel_call(functools.partial(row_kernel, False), row_msg, [tail])(cols, teacher_exp)
    rows = exchange(rows, "head")
    cols = kernel_call(functools.partial(col_kernel, False), col_msg, [tail])(rows, teacher_exp)
    cols = exchange(cols, "batch")
    cols, student_piece = tie(cols, student_piece)

    rows, col_scale = kernel_call(
        last_row_kernel, (row_msg_two, shape((8, columns))), [tail, tail]
    )(cols, teacher_exp, logits)
    rows = exchange(rows, "head")
    teacher_pull = kernel_call(pull_kernel, shape((4, total // 4, feature_dim)))(
        col_scale, teacher_exp, back
    )
    piece = pick(teacher_pull, y_index)
    for step in (1, 2, 3):
        pairs = [(i, i // 4 * 4 + (i + step) % 4) for i in range(32)]
        piece = piece + lax.ppermute(pick(teacher_pull, (y_index + step) % 4), "head", pairs)
    rows, piece = tie(rows, piece)

    part = shape((4, 2, share_rows, columns))
    keep, send, loss_part, row_scale = kernel_call(
        grad_kernel,
        (part, part, shape((1, 1, LANES)), shape((total // LANES, LANES))),
        [tail, tail, pltpu.VMEM((total, 512), BF16)],
        scalars=1,
    )(
        core.reshape(1), rows, partition, col_scale, teacher_exp, student_exp, flip, weight,
        weight_inv,
    )
    parts = keep + lax.ppermute(send, "batch", [(i, i ^ 1) for i in range(16)])
    held = pick(parts, x_index)
    for step in (1, 2, 3):
        pairs = [(i, (i + 4 * step) % 16) for i in range(16)]
        held = held + lax.ppermute(pick(parts, (x_index + step) % 4), "batch", pairs)

    piece = jnp.sum(
        exchange(piece.reshape(8, total // 32, feature_dim), "head", z_groups), axis=0
    )
    first = y_index * (total // 4) + (head_index // 4) * (total // 32)

    def cut(values):
        return lax.dynamic_slice_in_dim(values, first, total // 32, 0)

    piece = (
        student_piece / cut(partition.reshape(-1))[:, None]
        - piece * cut(row_scale.reshape(-1))[:, None]
    ) * (1.0 / STUDENT_TEMP)
    unit_piece = cut(unit)
    inner = jnp.sum(unit_piece * piece, axis=1, keepdims=True)
    piece = cut(inverse)[:, 0:1] * (piece - unit_piece * inner)
    piece = share(piece, "head", z_groups, 8).reshape(total // 4, feature_dim)
    piece, held = tie(piece, held)
    keep, send = pick(held, z_high), pick(held, 1 - z_high)
    grad_weight = keep + lax.ppermute(send, "batch", [(i, i ^ 2) for i in range(16)])
    grad_rows = share(piece, "head", y_groups, 4).reshape(view_count, masked_count, feature_dim)
    losses = share(loss_part[0], "batch", None, 16)
    loss = jnp.sum(losses, axis=0)[0, 0] / (total * lax.axis_size("batch"))
    return (grad_rows, grad_weight, loss)


def solution(mesh):
    in_specs = (P("batch", None, None), P("batch", None, None), P("batch", None), P(None, "head"))
    out_specs = (P("batch", None, None), P("batch", "head"), P())
    return jax.shard_map(
        per_device, mesh=mesh, in_specs=in_specs, out_specs=out_specs, check_vma=False
    )
```

time: 1510 us -> 342 us (0.23)
  the two profiles are of different devices: /device:TPU:120 before, /device:TPU:1 now
where the time goes in v2:
time: 342 us; the launch traced here: 340 us
  waiting for transfers between devices  127 us (37%)
  starting transfers between devices  106 us (31%)
  blocking collectives  39.9 us (12%)
  local copies, waits for them, and re-layouts  31 us (9%)
  Pallas kernels  16.3 us (5%)
  between operations  15.6 us (5%)
  other arithmetic  4.51 us (1%)
    all_to_all x8, starting transfers between devices, exchange(): return lax.all_to_all(blocks, axis, 0, 0, axis_index_groups=groups)  65.7 us
    reduce_scatter x1, waiting for transfers between devices, per_device(): lax.psum_scatter(student_piece.reshape(8, total // 32, feature_dim), 'hea...  59.4 us
    all_to_all x8, waiting for transfers between devices, exchange(): return lax.all_to_all(blocks, axis, 0, 0, axis_index_groups=groups)  59.3 us
    all_to_all x2, blocking collectives, exchange(): return lax.all_to_all(blocks, axis, 0, 0, axis_index_groups=groups)  39.9 us
    unnamed x39, local copies, waits for them, and re-layouts  28.5 us
    pallas_call x9, Pallas kernels, call(): pl.pallas_call(body, out_shape=out_shape, in_specs=specs, out_specs=jax.t...  16.3 us
    ppermute x1, starting transfers between devices, per_device(): lax.ppermute(send, 'batch', [(i, i ^ 2) for i in range(16)])  11.9 us
    ppermute x1, starting transfers between devices, per_device(): parts = keep + lax.ppermute(send, 'batch', [(i, i ^ 1) for i in range(16)])  9.57 us
  transfers between devices with their start and end apart: 18, of which 10 were waited for; matrix products, arithmetic and copies ran while one was open for 2% of the time, Pallas kernels for 2%

profile of v2, /device:TPU:1, one launch (start us, length us, event | category | flops | bytes accessed | tf_op | source)
XLA Modules:
  0.0 340.3 jit_solution(10448427107912812391)
XLA Ops:
  10.1 2.6 shard_map.67
  14.7 19.1 %all-to-all-start = ((f32[16,16,128]{2,1,0:T(8,128)}), f32[16,16,128]{2,1,0:T(8,128)S(1)}, u32[]{:S(2)}, u32[]{:S(2)}) async-start(f32[16,16,128]{2,1,0:T(8,128)} %get-tuple-element.37), calls=%async_computation | async-start | bytes 262144 | tf_op jit(solution)/shard_map/all_to_all | solution.py:242
  35.5 3.9 %shard_map.68 = (f32[512,256]{1,0:T(8,128)S(1)}, f32[512,128]{1,0:T(8,128)S(1)}, bf16[256,512]{1,0:T(8,128)(2,1)S(1)}, bf16[2048,256]{1,0:T(8,128)(2,1)S(1)}, f3...) custom-call(s32[4,128]{1,0:T(4,128)S(1)} %copy-done.15, ...), custom_call_target="tpu_custom_call" | custom-call | tf_op jit(solution)/shard_map/pallas_call | solution.py:25
  44.3 4.4 %all-to-all-done.refs_0_ = f32[16,16,128]{2,1,0:T(8,128)S(1)} async-done(((f32[16,16,128]{2,1,0:T(8,128)}), f32[16,16,128]{2,1,0:T(8,128)S(1)}, u32[]{:S(2)}, u32[]{:S(2)}) %all-to-all-start) | async-done | bytes 131104 | tf_op jit(solution)/shard_map/all_to_all | solution.py:242
  51.6 21.1 %all_to_all.50.rows_ref = f32[32,8,128]{2,1,0:T(8,128)S(1)} all-to-all(f32[32,8,128]{2,1,0:T(8,128)S(1)} %shard_map.69), channel_id=1, replica_groups=mesh['batch'=16,'head'=32] {'head'}, dimensions={0} | all-to-all | bytes 262144 | tf_op jit(solution)/shard_map/all_to_all | solution.py:242
  73.8 11.2 %all-to-all-start.2 = ((f32[16,16,128]{2,1,0:T(8,128)}), f32[16,16,128]{2,1,0:T(8,128)S(1)}, u32[]{:S(2)}, u32[]{:S(2)}) async-start(f32[16,16,128]{2,1,0:T(8,128)} %get-tuple-element.40), calls=%async_computation.2 | async-start | bytes 262144 | tf_op jit(solution)/shard_map/all_to_all | solution.py:242
  85.0 14.9 %all-to-all-done.2.refs_0_ = f32[16,16,128]{2,1,0:T(8,128)S(1)} async-done(((f32[16,16,128]{2,1,0:T(8,128)}), f32[16,16,128]{2,1,0:T(8,128)S(1)}, u32[]{:S(2)}, u32[]{:S(2)}) %all-to-all-start.2) | async-done | bytes 131104 | tf_op jit(solution)/shard_map/all_to_all | solution.py:242
  102.8 18.8 %all_to_all.51.rows_ref = f32[32,4,128]{2,1,0:T(4,128)S(1)} all-to-all(f32[32,4,128]{2,1,0:T(4,128)S(1)} %shard_map.71), channel_id=1, replica_groups=mesh['batch'=16,'head'=32] {'head'}, dimensions={0} | all-to-all | bytes 131072 | tf_op jit(solution)/shard_map/all_to_all | solution.py:242
  122.8 5.2 %all-to-all-start.4 = ((f32[16,16,128]{2,1,0:T(8,128)}), f32[16,16,128]{2,1,0:T(8,128)S(1)}, u32[]{:S(2)}, u32[]{:S(2)}) async-start(f32[16,16,128]{2,1,0:T(8,128)} %shard_map.72), calls=%async_computation.5 | async-start | bytes 262144 | tf_op jit(solution)/shard_map/all_to_all | solution.py:242
  128.7 59.4 %reduce-scatter.5.cloned.1.call-done = f32[1,16,256]{2,1,0:T(8,128)} async-done(((f32[8,16,256]{2,1,0:T(8,128)}), f32[1,16,256]{2,1,0:T(8,128)}) %reduce-scatter.5.cloned.1.call-update) | async-done | bytes 16400 | tf_op jit(solution)/shard_map/reduce_scatter | solution.py:309
  194.3 5.2 %all-to-all-start.5 = ((f32[32,8,128]{2,1,0:T(8,128)}), f32[32,8,128]{2,1,0:T(8,128)S(1)}, u32[]{:S(2)}, u32[]{:S(2)}) async-start(f32[32,8,128]{2,1,0:T(8,128)} %get-tuple-element.48), calls=%async_computation.7 | async-start | bytes 262144 | tf_op jit(solution)/shard_map/all_to_all | solution.py:242
  203.1 4.3 %collective-permute-start.2 = (f32[128,256]{1,0:T(8,128)S(1)}, f32[128,256]{1,0:T(8,128)S(1)}, u32[]{:S(2)}, u32[]{:S(2)}) collective-permute-start(f32[128,256]{1,0:T(8,128)S(1)} %get-tuple-element.67), channel_id=1, source_target_pairs={{0,3},{1,0},{2,1},{3,2},{4,7},{5,4},{6,5},{7,6},{8,11},{9,8},{10,9... | collective-permute-start | bytes 393224 | tf_op jit(solution)/shard_map/ppermute | solution.py:328
  207.5 2.5 collective-permute-start.1
  210.0 2.5 collective-permute-start
  212.5 2.6 collective-permute-done.1
  215.1 2.2 collective-permute-done
  218.0 2.2 copy-done.5
  222.4 2.9 shard_map.75
  225.3 9.6 %collective-permute-start.3 = (f32[4,2,16,2048]{3,2,1,0:T(8,128)}, f32[4,2,16,2048]{3,2,1,0:T(8,128)S(1)}, u32[]{:S(2)}, u32[]{:S(2)}) collective-permute-start(f32[4,2,16,2048]{3,2,1,0:T(8,128)} %get-tuple-element.59), channel_id=1, source_target_pairs={{0,32},{32,0},{64,96},{96,64},{128,160},{160,128},{192,224},{224,1... | collective-permute-start | bytes 3145736 | tf_op jit(solution)/shard_map/ppermute | solution.py:341
  234.9 9.2 %all-to-all-start.6 = ((f32[8,16,256]{2,1,0:T(8,128)}), f32[8,16,256]{2,1,0:T(8,128)S(1)}, u32[]{:S(2)}, u32[]{:S(2)}) async-start(f32[8,16,256]{2,1,0:T(8,128)} %bitcast.9), calls=%async_computation.8 | async-start | bytes 262144 | tf_op jit(solution)/shard_map/all_to_all | solution.py:242
  244.3 10.3 %all-to-all-done.6 = f32[8,16,256]{2,1,0:T(8,128)S(1)} async-done(((f32[8,16,256]{2,1,0:T(8,128)}), f32[8,16,256]{2,1,0:T(8,128)S(1)}, u32[]{:S(2)}, u32[]{:S(2)}) %all-to-all-start.6) | async-done | bytes 131104 | tf_op jit(solution)/shard_map/all_to_all | solution.py:242
  257.1 4.3 %collective-permute-start.6 = (f32[2,16,2048]{2,1,0:T(8,128)S(1)}, f32[2,16,2048]{2,1,0:T(8,128)S(1)}, u32[]{:S(2)}, u32[]{:S(2)}) collective-permute-start(f32[2,16,2048]{2,1,0:T(8,128)S(1)} %get-tuple-element.64), channel_id=1, source_target_pairs={{0,384},{32,416},{64,448},{96,480},{128,0},{160,32},{192,64},{224,... | collective-permute-start | bytes 786440 | tf_op jit(solution)/shard_map/ppermute | solution.py:345
  261.4 2.5 collective-permute-start.5
  263.9 2.5 collective-permute-start.4
  268.8 5.4 %all-to-all-start.7 = ((f32[8,16,256]{2,1,0:T(8,128)}), f32[8,16,256]{2,1,0:T(8,128)S(1)}, u32[]{:S(2)}, u32[]{:S(2)}) async-start(f32[8,16,256]{2,1,0:T(8,128)} %broadcast_in_dim.8), calls=%async_computation.9 | async-start | bytes 262144 | tf_op jit(solution)/shard_map/all_to_all | solution.py:242
  274.3 3.0 collective-permute-done.4
  277.3 7.3 %all-to-all-done.7 = f32[8,16,256]{2,1,0:T(8,128)S(1)} async-done(((f32[8,16,256]{2,1,0:T(8,128)}), f32[8,16,256]{2,1,0:T(8,128)S(1)}, u32[]{:S(2)}, u32[]{:S(2)}) %all-to-all-start.7) | async-done | bytes 131104 | tf_op jit(solution)/shard_map/all_to_all | solution.py:242
  284.6 11.9 %collective-permute-start.7 = (f32[16,2048]{1,0:T(8,128)S(1)}, f32[16,2048]{1,0:T(8,128)S(1)}, u32[]{:S(2)}, u32[]{:S(2)}) collective-permute-start(f32[16,2048]{1,0:T(8,128)S(1)} %dynamic-slice_bitcast_fusion.3), channel_id=1, source_target_pairs={{0,64},{32,96},{64,0},{96,32},{128,192},{160,224},{192,128},{224,1... | collective-permute-start | bytes 393224 | tf_op jit(solution)/shard_map/ppermute | solution.py:365
  297.1 7.0 %all-to-all-start.9 = ((f32[16,1,128]{2,1,0:T(1,128)}), f32[16,1,128]{2,1,0:T(1,128)S(1)}, u32[]{:S(2)}, u32[]{:S(2)}) async-start(f32[16,1,128]{2,1,0:T(1,128)} %broadcast_in_dim.11), calls=%async_computation.11 | async-start | bytes 16384 | tf_op jit(solution)/shard_map/all_to_all | solution.py:242
  304.2 14.1 %all-to-all-done.9 = f32[16,1,128]{2,1,0:T(1,128)S(1)} async-done(((f32[16,1,128]{2,1,0:T(1,128)}), f32[16,1,128]{2,1,0:T(1,128)S(1)}, u32[]{:S(2)}, u32[]{:S(2)}) %all-to-all-start.9) | async-done | bytes 8224 | tf_op jit(solution)/shard_map/all_to_all | solution.py:242
  319.2 3.5 %all-to-all-start.8 = ((f32[4,128,256]{2,1,0:T(8,128)}), f32[4,128,256]{2,1,0:T(8,128)S(1)}, u32[]{:S(2)}, u32[]{:S(2)}) async-start(f32[4,128,256]{2,1,0:T(8,128)} %broadcast_in_dim.9), calls=%async_computation.10 | async-start | bytes 1048576 | tf_op jit(solution)/shard_map/all_to_all | solution.py:242
  323.3 8.2 %all-to-all-done.8 = f32[4,128,256]{2,1,0:T(8,128)S(1)} async-done(((f32[4,128,256]{2,1,0:T(8,128)}), f32[4,128,256]{2,1,0:T(8,128)S(1)}, u32[]{:S(2)}, u32[]{:S(2)}) %all-to-all-start.8) | async-done | bytes 524320 | tf_op jit(solution)/shard_map/all_to_all | solution.py:242
  (73 shorter events, 41.0 us)
Async XLA Ops:
  7.2 1.2 copy-start.8
  12.7 2.0 copy-start
  14.7 34.0 %all-to-all-start = ((f32[16,16,128]{2,1,0:T(8,128)}), f32[16,16,128]{2,1,0:T(8,128)S(1)}, u32[]{:S(2)}, u32[]{:S(2)}) async-start(f32[16,16,128]{2,1,0:T(8,128)} %get-tuple-element.37), calls=%async_computation | async-start | bytes 262144 | tf_op jit(solution)/shard_map/all_to_all | solution.py:242
  33.7 51.2 %reduce-scatter.3.cloned.1.call-start = ((), (), s32[]{:S(2)}) async-start(), calls=%async_computation.12 | async-start | bytes 655360 | tf_op jit(solution)/shard_map/reduce_scatter | solution.py:301
  33.8 1.0 copy-start.13
  39.4 2.0 copy-start.6
  41.5 2.0 copy-start.10
  48.7 2.2 copy-start.1
  73.8 26.1 %all-to-all-start.2 = ((f32[16,16,128]{2,1,0:T(8,128)}), f32[16,16,128]{2,1,0:T(8,128)S(1)}, u32[]{:S(2)}, u32[]{:S(2)}) async-start(f32[16,16,128]{2,1,0:T(8,128)} %get-tuple-element.40), calls=%async_computation.2 | async-start | bytes 262144 | tf_op jit(solution)/shard_map/all_to_all | solution.py:242
  99.9 2.2 copy-start.2
  122.8 65.3 %all-to-all-start.4 = ((f32[16,16,128]{2,1,0:T(8,128)}), f32[16,16,128]{2,1,0:T(8,128)S(1)}, u32[]{:S(2)}, u32[]{:S(2)}) async-start(f32[16,16,128]{2,1,0:T(8,128)} %shard_map.72), calls=%async_computation.5 | async-start | bytes 262144 | tf_op jit(solution)/shard_map/all_to_all | solution.py:242
  127.9 60.1 %reduce-scatter.5.cloned.1.call-start = ((), (), s32[]{:S(2)}) async-start(), calls=%async_computation.13 | async-start | bytes 147456 | tf_op jit(solution)/shard_map/reduce_scatter | solution.py:309
  188.1 2.2 copy-start.3
  190.3 2.2 copy-start.11
  192.4 25.6 %copy-start.9 = (bf16[256,2048]{1,0:T(8,128)(2,1)S(1)}, bf16[256,2048]{1,0:T(8,128)(2,1)}, u32[]{:S(2)}) copy-start(bf16[256,2048]{1,0:T(8,128)(2,1)} %weight_ref.3) | copy-start | bytes 3145732
  194.3 23.8 %all-to-all-start.5 = ((f32[32,8,128]{2,1,0:T(8,128)}), f32[32,8,128]{2,1,0:T(8,128)S(1)}, u32[]{:S(2)}, u32[]{:S(2)}) async-start(f32[32,8,128]{2,1,0:T(8,128)} %get-tuple-element.48), calls=%async_computation.7 | async-start | bytes 262144 | tf_op jit(solution)/shard_map/all_to_all | solution.py:242
  199.5 2.2 copy-start.4
  203.1 9.4 %collective-permute-start.2 = (f32[128,256]{1,0:T(8,128)S(1)}, f32[128,256]{1,0:T(8,128)S(1)}, u32[]{:S(2)}, u32[]{:S(2)}) collective-permute-start(f32[128,256]{1,0:T(8,128)S(1)} %get-tuple-element.67), channel_id=1, source_target_pairs={{0,3},{1,0},{2,1},{3,2},{4,7},{5,4},{6,5},{7,6},{8,11},{9,8},{10,9... | collective-permute-start | bytes 393224 | tf_op jit(solution)/shard_map/ppermute | solution.py:328
  207.5 7.6 %collective-permute-start.1 = (f32[128,256]{1,0:T(8,128)S(1)}, f32[128,256]{1,0:T(8,128)S(1)}, u32[]{:S(2)}, u32[]{:S(2)}) collective-permute-start(f32[128,256]{1,0:T(8,128)S(1)} %get-tuple-element.68), channel_id=1, source_target_pairs={{0,2},{1,3},{2,0},{3,1},{4,6},{5,7},{6,4},{7,5},{8,10},{9,11},{10,... | collective-permute-start | bytes 393224 | tf_op jit(solution)/shard_map/ppermute | solution.py:328
  210.0 7.3 %collective-permute-start = (f32[128,256]{1,0:T(8,128)S(1)}, f32[128,256]{1,0:T(8,128)S(1)}, u32[]{:S(2)}, u32[]{:S(2)}) collective-permute-start(f32[128,256]{1,0:T(8,128)S(1)} %get-tuple-element.66), channel_id=1, source_target_pairs={{0,1},{1,2},{2,3},{3,0},{4,5},{5,6},{6,7},{7,4},{8,9},{9,10},{10,1... | collective-permute-start | bytes 393224 | tf_op jit(solution)/shard_map/ppermute | solution.py:328
  218.0 2.2 copy-start.5
  220.2 2.2 copy-start.7
  225.3 41.1 %copy-start.18 = (f32[1,16,256]{2,1,0:T(8,128)S(1)}, f32[1,16,256]{2,1,0:T(8,128)}, u32[]{:S(2)}) copy-start(f32[1,16,256]{2,1,0:T(8,128)} %reduce-scatter.5.cloned.1.call-done) | copy-start | bytes 49156
  225.3 29.4 %collective-permute-start.3 = (f32[4,2,16,2048]{3,2,1,0:T(8,128)}, f32[4,2,16,2048]{3,2,1,0:T(8,128)S(1)}, u32[]{:S(2)}, u32[]{:S(2)}) collective-permute-start(f32[4,2,16,2048]{3,2,1,0:T(8,128)} %get-tuple-element.59), channel_id=1, source_target_pairs={{0,32},{32,0},{64,96},{96,64},{128,160},{160,128},{192,224},{224,1... | collective-permute-start | bytes 3145736 | tf_op jit(solution)/shard_map/ppermute | solution.py:341
  234.9 19.8 %all-to-all-start.6 = ((f32[8,16,256]{2,1,0:T(8,128)}), f32[8,16,256]{2,1,0:T(8,128)S(1)}, u32[]{:S(2)}, u32[]{:S(2)}) async-start(f32[8,16,256]{2,1,0:T(8,128)} %bitcast.9), calls=%async_computation.8 | async-start | bytes 262144 | tf_op jit(solution)/shard_map/all_to_all | solution.py:242
  257.1 17.2 %collective-permute-start.6 = (f32[2,16,2048]{2,1,0:T(8,128)S(1)}, f32[2,16,2048]{2,1,0:T(8,128)S(1)}, u32[]{:S(2)}, u32[]{:S(2)}) collective-permute-start(f32[2,16,2048]{2,1,0:T(8,128)S(1)} %get-tuple-element.64), channel_id=1, source_target_pairs={{0,384},{32,416},{64,448},{96,480},{128,0},{160,32},{192,64},{224,... | collective-permute-start | bytes 786440 | tf_op jit(solution)/shard_map/ppermute | solution.py:345
  261.4 12.8 %collective-permute-start.5 = (f32[2,16,2048]{2,1,0:T(8,128)S(1)}, f32[2,16,2048]{2,1,0:T(8,128)S(1)}, u32[]{:S(2)}, u32[]{:S(2)}) collective-permute-start(f32[2,16,2048]{2,1,0:T(8,128)S(1)} %get-tuple-element.65), channel_id=1, source_target_pairs={{0,256},{32,288},{64,320},{96,352},{128,384},{160,416},{192,448},{... | collective-permute-start | bytes 786440 | tf_op jit(solution)/shard_map/ppermute | solution.py:345
  263.9 13.3 %collective-permute-start.4 = (f32[2,16,2048]{2,1,0:T(8,128)S(1)}, f32[2,16,2048]{2,1,0:T(8,128)S(1)}, u32[]{:S(2)}, u32[]{:S(2)}) collective-permute-start(f32[2,16,2048]{2,1,0:T(8,128)S(1)} %get-tuple-element.63), channel_id=1, source_target_pairs={{0,128},{32,160},{64,192},{96,224},{128,256},{160,288},{192,320},{... | collective-permute-start | bytes 786440 | tf_op jit(solution)/shard_map/ppermute | solution.py:345
  268.8 15.7 %all-to-all-start.7 = ((f32[8,16,256]{2,1,0:T(8,128)}), f32[8,16,256]{2,1,0:T(8,128)S(1)}, u32[]{:S(2)}, u32[]{:S(2)}) async-start(f32[8,16,256]{2,1,0:T(8,128)} %broadcast_in_dim.8), calls=%async_computation.9 | async-start | bytes 262144 | tf_op jit(solution)/shard_map/all_to_all | solution.py:242
  284.6 38.1 %collective-permute-start.7 = (f32[16,2048]{1,0:T(8,128)S(1)}, f32[16,2048]{1,0:T(8,128)S(1)}, u32[]{:S(2)}, u32[]{:S(2)}) collective-permute-start(f32[16,2048]{1,0:T(8,128)S(1)} %dynamic-slice_bitcast_fusion.3), channel_id=1, source_target_pairs={{0,64},{32,96},{64,0},{96,32},{128,192},{160,224},{192,128},{224,1... | collective-permute-start | bytes 393224 | tf_op jit(solution)/shard_map/ppermute | solution.py:365
  297.1 21.2 %all-to-all-start.9 = ((f32[16,1,128]{2,1,0:T(1,128)}), f32[16,1,128]{2,1,0:T(1,128)S(1)}, u32[]{:S(2)}, u32[]{:S(2)}) async-start(f32[16,1,128]{2,1,0:T(1,128)} %broadcast_in_dim.11), calls=%async_computation.11 | async-start | bytes 16384 | tf_op jit(solution)/shard_map/all_to_all | solution.py:242
  319.2 12.3 %all-to-all-start.8 = ((f32[4,128,256]{2,1,0:T(8,128)}), f32[4,128,256]{2,1,0:T(8,128)S(1)}, u32[]{:S(2)}, u32[]{:S(2)}) async-start(f32[4,128,256]{2,1,0:T(8,128)} %broadcast_in_dim.9), calls=%async_computation.10 | async-start | bytes 1048576 | tf_op jit(solution)/shard_map/all_to_all | solution.py:242
  (5 other events, 4.2 us)
Sparse Core Ops, SparseCore 0:
  44.4 28.3 reduce-scatter.2
  131.6 56.4 reduce-scatter.4

commit v3 on v2

v3 whole, which is shorter than its diff:
```python
import functools

import jax
import jax.numpy as jnp
from jax import lax
from jax.experimental import pallas as pl
from jax.experimental.pallas import tpu as pltpu
from jax.sharding import PartitionSpec as P

TEACHER_TEMP = 0.07
STUDENT_TEMP = 0.1
EPSILON = 1e-06
LANES = 128
F32 = jnp.float32
BF16 = jnp.bfloat16
MIB = 1 << 20


def kernel_call(body, out_shape, scratch=(), limit=12, scalars=0, far=0):
    whole = pl.BlockSpec(memory_space=pltpu.VMEM)

    def call(*args):
        specs = [pl.BlockSpec(memory_space=pltpu.SMEM)] * scalars
        specs += [pl.BlockSpec(memory_space=pltpu.HBM)] * far
        specs += [whole] * (len(args) - scalars - far)
        return pl.pallas_call(
            body,
            out_shape=out_shape,
            in_specs=specs,
            out_specs=jax.tree.map(lambda _: whole, out_shape),
            scratch_shapes=list(scratch),
            compiler_params=pltpu.CompilerParams(vmem_limit_bytes=limit * MIB),
        )(*args)

    return call


def shape(dims, dtype=F32):
    return jax.ShapeDtypeStruct(dims, dtype)


def picked_unit(patches, positions):
    patch = lax.broadcasted_iota(jnp.int32, (patches.shape[0], positions.shape[1]), 0)
    onehot = (patch == positions).astype(F32).astype(BF16)
    rows = lax.dot_general(
        onehot, patches, (((0,), (0,)), ((), ())), preferred_element_type=F32
    )
    inverse = lax.rsqrt(jnp.sum(rows * rows, axis=1, keepdims=True) + EPSILON)
    return rows * inverse, inverse


def far_off(array):
    return pltpu.with_memory_space_constraint(array, pltpu.HBM)


def lane_tiles(row, count):
    return jnp.concatenate(
        [jnp.broadcast_to(row[i : i + 1, :], (8, LANES)) for i in range(count)], axis=1
    )


def column(row):
    return jnp.transpose(jnp.broadcast_to(row, (LANES, LANES)))


def fold(block):
    tiles = [block[:, i : i + LANES] for i in range(0, block.shape[1], LANES)]
    while len(tiles) > 1:
        tiles = [a + b for a, b in zip(tiles[::2], tiles[1::2])]
    return tiles[0]


def row_sums(partial):
    total = lax.dot_general(
        jnp.ones((8, LANES), F32),
        partial,
        (((1,), (1,)), ((), ())),
        precision=lax.Precision.HIGHEST,
        preferred_element_type=F32,
    )
    return jnp.concatenate(
        [total[0:1, i : i + LANES] for i in range(0, partial.shape[0], LANES)], axis=0
    )


def col_tiles(total):
    return jnp.concatenate(
        [total[:, i : i + LANES] for i in range(0, total.shape[1], LANES)], axis=0
    )


def start_kernel(
    places_ref, weight_hbm, teacher_hbm, student_hbm, index_ref,
    back_ref, inv_ref, teacher_exp_ref, msg_ref,
    own_unit_ref, own_inv_ref, flip_ref, logits_ref, student_exp_ref, part_ref,
    weight_ref, teacher_ref, student_ref, norm_ref, unit_ref, row_inv_ref, tail, sems,
):
    copies = [
        pltpu.make_async_copy(source, target, sems.at[i])
        for i, (source, target) in enumerate(
            [(weight_hbm, weight_ref), (teacher_hbm, teacher_ref), (student_hbm, student_ref)]
        )
    ]
    for copy in copies:
        copy.start()
    copies[0].wait()
    wide = weight_ref[...].astype(F32)
    inverse = lax.rsqrt(jnp.sum(wide * wide, axis=0, keepdims=True) + EPSILON)
    inv_ref[...] = inverse
    norm_ref[...] = (wide * inverse).astype(BF16)
    back_ref[...] = jnp.transpose(norm_ref[...])
    copies[1].wait()
    total = jnp.zeros((1, weight_ref.shape[1]), F32)
    for view in range(teacher_ref.shape[0]):
        unit, _ = picked_unit(teacher_ref[view], index_ref[view : view + 1, :])
        logits = jnp.dot(unit.astype(BF16), norm_ref[...], preferred_element_type=F32)
        block = jnp.exp(logits * (1.0 / TEACHER_TEMP))
        teacher_exp_ref[view * LANES : (view + 1) * LANES, :] = block
        total += jnp.sum(block, axis=0, keepdims=True)
    msg_ref[...] = jnp.broadcast_to(col_tiles(total)[None], msg_ref.shape)
    copies[2].wait()
    for view in range(student_ref.shape[0]):
        rows = slice(view * LANES, (view + 1) * LANES)
        unit, inverse = picked_unit(student_ref[view], index_ref[view : view + 1, :])
        unit_ref[rows, :] = unit
        row_inv_ref[rows, :] = jnp.broadcast_to(inverse, (LANES, LANES))
        narrow = unit.astype(BF16)
        flip_ref[:, rows] = jnp.transpose(narrow)
        logits = jnp.dot(narrow, norm_ref[...], preferred_element_type=F32)
        block = jnp.exp(logits * (1.0 / STUDENT_TEMP))
        logits_ref[rows, :] = logits
        student_exp_ref[rows, :] = block
        tail[rows, :] = fold(block)
    part_ref[...] = row_sums(tail[...])
    own = pl.ds(pl.multiple_of(places_ref[3], 16), own_unit_ref.shape[0])
    own_unit_ref[...] = unit_ref[own, :]
    own_inv_ref[...] = row_inv_ref[own, :]


def row_kernel(has_extra, *refs):
    if has_extra:
        cols_ref, exp_ref, extra_ref, msg_ref, tail = refs
    else:
        cols_ref, exp_ref, msg_ref, tail = refs
    scale = lane_tiles(1.0 / jnp.sum(cols_ref[...], axis=0), cols_ref.shape[1])

    def step(i, carry):
        start = pl.multiple_of(i * 8, 8)
        tail[pl.ds(start, 8), :] = fold(exp_ref[pl.ds(start, 8), :] * scale)
        return carry

    lax.fori_loop(0, exp_ref.shape[0] // 8, step, 0, unroll=8)
    out = row_sums(tail[...])
    if has_extra:
        out = jnp.concatenate([out, extra_ref[...]], axis=0)
    msg_ref[...] = jnp.broadcast_to(out[None], msg_ref.shape)


def col_kernel(has_extra, rows_ref, exp_ref, *refs):
    if has_extra:
        msg_ref, extra_ref, scale_ref = refs
    else:
        msg_ref, scale_ref = refs
    total = jnp.sum(rows_ref[...], axis=0)
    if has_extra:
        extra_ref[...] = total[4:8, :]
    scale = 1.0 / total[0:4, :]
    for j in range(4):
        scale_ref[j * LANES : (j + 1) * LANES, :] = column(scale[j : j + 1, :])
    count = exp_ref.shape[1] // LANES

    def step(i, sums):
        start = pl.multiple_of(i * 8, 8)
        factor = scale_ref[pl.ds(start, 8), :]
        return tuple(
            sums[k] + exp_ref[pl.ds(start, 8), k * LANES : (k + 1) * LANES] * factor
            for k in range(count)
        )

    sums = lax.fori_loop(
        0, exp_ref.shape[0] // 8, step, (jnp.zeros((8, LANES), F32),) * count, unroll=8
    )
    total = jnp.concatenate([jnp.sum(s, axis=0, keepdims=True) for s in sums], axis=0)
    msg_ref[...] = jnp.broadcast_to(total[None], msg_ref.shape)


def last_row_kernel(cols_ref, exp_ref, logits_ref, msg_ref, scale_ref, tail, weighted):
    small = 1.0 / jnp.sum(cols_ref[...], axis=0)
    scale = lane_tiles(small, cols_ref.shape[1])
    scale_ref[...] = scale

    def step(i, carry):
        start = pl.multiple_of(i * 8, 8)
        scaled = exp_ref[pl.ds(start, 8), :] * scale
        tail[pl.ds(start, 8), :] = fold(scaled)
        weighted[pl.ds(start, 8), :] = fold(scaled * logits_ref[pl.ds(start, 8), :])
        return carry

    lax.fori_loop(0, exp_ref.shape[0] // 8, step, 0, unroll=4)
    out = jnp.concatenate([row_sums(tail[...]), row_sums(weighted[...])], axis=0)
    msg_ref[...] = jnp.broadcast_to(out[None], msg_ref.shape)


def grad_kernel(
    places_ref, rows_ref, partition_ref, scale_ref, exp_ref, student_ref, flip_ref, back_ref,
    weight_ref, inv_ref, keep_ref, send_ref, pull_ref, factor, softener, logits,
):
    total = jnp.sum(rows_ref[...], axis=0)
    partition = partition_ref[...]
    scale = 1.0 / total[0:4, :]
    losses = jnp.log(partition) - scale * total[4:8, :] * (1.0 / STUDENT_TEMP)
    loss = jnp.sum(jnp.sum(losses, axis=1, keepdims=True), axis=0, keepdims=True)
    columns = exp_ref.shape[1]
    for ref in (keep_ref, send_ref):
        ref[:, :, :, columns:] = jnp.broadcast_to(loss[None, None], ref.shape[:3] + (LANES,))
    softener_rows = 1.0 / partition
    for j in range(4):
        rows = slice(j * LANES, (j + 1) * LANES)
        factor[rows, :] = column(scale[j : j + 1, :])
        softener[rows, :] = column(softener_rows[j : j + 1, :])
    width = logits.shape[1]
    core, x_index, z_high = places_ref[0], places_ref[1], places_ref[2]
    wide = (LANES, width)
    for block in range(columns // width):
        cols = slice(block * width, (block + 1) * width)
        for j in range(4):
            rows = slice(j * LANES, (j + 1) * LANES)
            soft = jnp.concatenate([softener[rows, :]] * (width // LANES), axis=1)
            hard = jnp.concatenate([factor[rows, :]] * (width // LANES), axis=1)
            targets = hard * (exp_ref[rows, cols] * scale_ref[0:1, cols])
            logits[rows, :] = (
                (student_ref[rows, cols] * soft - targets) * (1.0 / STUDENT_TEMP)
            ).astype(BF16)
        pull = jnp.dot(logits[...], back_ref[cols, :], preferred_element_type=F32)
        pull = pull.reshape(pull_ref.shape)
        pull_ref[...] = pull if block == 0 else pull_ref[...] + pull
        unit = jnp.dot(flip_ref[...], logits[...], preferred_element_type=F32)
        inverse = inv_ref[:, cols]
        weight_unit = weight_ref[:, cols].astype(F32) * inverse
        inner = jnp.sum(weight_unit * unit, axis=0, keepdims=True)
        full = (inverse * (unit - weight_unit * inner)).reshape(4, 2, 2, 16, width)
        first, second = full[:, :, 0], full[:, :, 1]
        for x in range(4):
            for z in range(2):
                place = ((x - x_index) & 3, z ^ z_high)
                keep_ref[place + (slice(None), cols)] = jnp.where(
                    core == 0, first[x, z], second[x, z]
                )
                send_ref[place + (slice(None), cols)] = jnp.where(
                    core == 0, second[x, z], first[x, z]
                )


def finish_kernel(blocks_ref, unit_ref, inv_ref, copies_ref):
    pull = jnp.sum(blocks_ref[...], axis=0)
    unit = unit_ref[...]
    inner = jnp.sum(unit * pull, axis=1, keepdims=True)
    rows = inv_ref[:, 0:1] * (pull - unit * inner)
    copies_ref[...] = jnp.broadcast_to(rows[None], copies_ref.shape)


def exchange(blocks, axis, groups=None):
    return lax.all_to_all(blocks, axis, 0, 0, axis_index_groups=groups)


def share(block, axis, groups, count):
    return exchange(jnp.broadcast_to(block[None], (count,) + block.shape), axis, groups)


def tie(*values):
    return lax.optimization_barrier(values)


def per_device(student_patches, teacher_patches, mask_index, weight):
    view_count, masked_count = mask_index.shape
    feature_dim, columns = weight.shape
    total = view_count * masked_count
    share_rows = feature_dim // 16
    batch_index = lax.axis_index("batch")
    head_index = lax.axis_index("head")
    first = (head_index & 3) * (total // 4) + (head_index >> 2) * (total // 32)
    places = jnp.stack([batch_index & 1, batch_index >> 2, (batch_index >> 1) & 1, first])
    y_groups = [[4 * z + y for y in range(4)] for z in range(8)]
    z_groups = [[4 * z + y for z in range(8)] for y in range(4)]
    col_msg = shape((16, columns // LANES, LANES))
    row_msg = shape((32, total // LANES, LANES))
    row_msg_two = shape((32, 2 * total // LANES, LANES))
    tail = pltpu.VMEM((total, LANES), F32)

    (
        back, weight_inv, teacher_exp, cols,
        unit, inverse, flip, logits, student_exp, partition_part,
    ) = kernel_call(
        start_kernel,
        (
            shape((columns, feature_dim), BF16),
            shape((1, columns)),
            shape((total, columns)),
            col_msg,
            shape((total // 32, feature_dim)),
            shape((total // 32, LANES)),
            shape((feature_dim, total), BF16),
            shape((total, columns)),
            shape((total, columns)),
            shape((total // LANES, LANES)),
        ),
        [
            pltpu.VMEM(weight.shape, BF16),
            pltpu.VMEM(teacher_patches.shape, BF16),
            pltpu.VMEM(student_patches.shape, BF16),
            pltpu.VMEM((feature_dim, columns), BF16),
            pltpu.VMEM((total, feature_dim), F32),
            tail,
            tail,
            pltpu.SemaphoreType.DMA((3,)),
        ],
        scalars=1,
        far=3,
        limit=16,
    )(
        places, far_off(weight), far_off(teacher_patches), far_off(student_patches), mask_index
    )
    cols = exchange(cols, "batch")
    rows = kernel_call(functools.partial(row_kernel, True), row_msg_two, [tail])(
        cols, teacher_exp, partition_part
    )
    rows = exchange(rows, "head")
    cols, partition = kernel_call(
        functools.partial(col_kernel, True), (col_msg, shape((total // LANES, LANES))), [tail]
    )(rows, teacher_exp)
    cols = exchange(cols, "batch")
    rows = kernel_call(functools.partial(row_kernel, False), row_msg, [tail])(cols, teacher_exp)
    rows = exchange(rows, "head")
    cols = kernel_call(functools.partial(col_kernel, False), col_msg, [tail])(rows, teacher_exp)
    cols = exchange(cols, "batch")
    rows, col_scale = kernel_call(
        last_row_kernel, (row_msg_two, shape((8, columns))), [tail, tail]
    )(cols, teacher_exp, logits)
    rows = exchange(rows, "head")

    part = shape((4, 2, share_rows, columns + LANES))
    keep, send, pull = kernel_call(
        grad_kernel,
        (part, part, shape((4, total // 4, feature_dim))),
        [tail, tail, pltpu.VMEM((total, 512), BF16)],
        scalars=1,
        limit=16,
    )(
        places, rows, partition, col_scale, teacher_exp, student_exp, flip, back, weight,
        weight_inv,
    )
    parts = keep + lax.ppermute(send, "batch", [(i, i ^ 1) for i in range(16)])
    parts, pull = tie(parts, pull)
    piece = jnp.sum(exchange(pull, "head", y_groups), axis=0)

    held = parts[0]
    for step in (1, 2, 3):
        pairs = [(i, (i + 4 * step) % 16) for i in range(16)]
        held = held + lax.ppermute(parts[step], "batch", pairs)

    piece = kernel_call(finish_kernel, shape((8, total // 32, feature_dim)))(
        exchange(piece.reshape(8, total // 32, feature_dim), "head", z_groups), unit, inverse
    )
    piece = exchange(piece, "head", z_groups).reshape(total // 4, feature_dim)
    grad_weight = held[0] + lax.ppermute(held[1], "batch", [(i, i ^ 2) for i in range(16)])
    grad_rows = share(piece, "head", y_groups, 4).reshape(view_count, masked_count, feature_dim)
    loss = grad_weight[0, columns] / (total * lax.axis_size("batch"))
    return (grad_rows, grad_weight[:, :columns], loss)


def solution(mesh):
    in_specs = (P("batch", None, None), P("batch", None, None), P("batch", None), P(None, "head"))
    out_specs = (P("batch", None, None), P("batch", "head"), P())
    return jax.shard_map(
        per_device, mesh=mesh, in_specs=in_specs, out_specs=out_specs, check_vma=False
    )
```

time: 342 us -> 222 us (0.65)
  the two profiles are of different devices: /device:TPU:1 before, /device:TPU:32 now
where the time goes in v3:
time: 222 us; the launch traced here: 221 us
  blocking collectives  132 us (59%)
  waiting for transfers between devices  37.3 us (17%)
  starting transfers between devices  31.1 us (14%)
  Pallas kernels  13.5 us (6%)
  local copies, waits for them, and re-layouts  3.56 us (2%)
  between operations  2.55 us (1%)
    all_to_all x6, blocking collectives, exchange(): return lax.all_to_all(blocks, axis, 0, 0, axis_index_groups=groups)  132 us
    all_to_all x4, waiting for transfers between devices, exchange(): return lax.all_to_all(blocks, axis, 0, 0, axis_index_groups=groups)  31.5 us
    all_to_all x4, starting transfers between devices, exchange(): return lax.all_to_all(blocks, axis, 0, 0, axis_index_groups=groups)  17.6 us
    pallas_call x8, Pallas kernels, call(): pl.pallas_call(body, out_shape=out_shape, in_specs=specs, out_specs=jax.t...  13.5 us
    ppermute x3, starting transfers between devices, per_device(): held = held + lax.ppermute(parts[step], 'batch', pairs)  8.97 us
  transfers between devices with their start and end apart: 9, of which 6 were waited for; matrix products, arithmetic and copies ran while one was open for 1% of the time, Pallas kernels for 0%

profile of v3, /device:TPU:32, one launch (start us, length us, event | category | flops | bytes accessed | tf_op | source)
XLA Modules:
  0.0 221.1 jit_solution(10907013779115525694)
XLA Ops:
  0.7 0.7 copy-done.1
  1.4 5.9 %shard_map.67 = (bf16[2048,256]{1,0:T(8,128)(2,1)S(1)}, f32[1,2048]{1,0:T(1,128)S(1)}, f32[512,2048]{1,0:T(8,128)S(1)}, f32[16,16,128]{2,1,0:T(8,128)S(1)}, f32[...) custom-call(s32[4]{0:T(128)S(1)} %pad_add_fusion.places_ref, ...), custom_call_target="tpu_custom_call" | custom-call | tf_op jit(solution)/shard_map/pallas_call | solution.py:26
  7.3 36.2 %all_to_all.50.refs_0_ = f32[16,16,128]{2,1,0:T(8,128)S(1)} all-to-all(f32[16,16,128]{2,1,0:T(8,128)S(1)} %get-tuple-element.22), channel_id=1, replica_groups=mesh['batch'=16,'head'=32] {'batch'}, dimensions={0} | all-to-all | bytes 262144 | tf_op jit(solution)/shard_map/all_to_all | solution.py:263
  43.5 0.7 shard_map.68
  44.2 18.9 %all_to_all.51.rows_ref = f32[32,8,128]{2,1,0:T(8,128)S(1)} all-to-all(f32[32,8,128]{2,1,0:T(8,128)S(1)} %shard_map.68), channel_id=1, replica_groups=mesh['batch'=16,'head'=32] {'head'}, dimensions={0} | all-to-all | bytes 262144 | tf_op jit(solution)/shard_map/all_to_all | solution.py:263
  63.6 22.2 %all_to_all.52.refs_0_ = f32[16,16,128]{2,1,0:T(8,128)S(1)} all-to-all(f32[16,16,128]{2,1,0:T(8,128)S(1)} %get-tuple-element.25), channel_id=1, replica_groups=mesh['batch'=16,'head'=32] {'batch'}, dimensions={0} | all-to-all | bytes 262144 | tf_op jit(solution)/shard_map/all_to_all | solution.py:263
  85.8 0.7 shard_map.70
  86.5 15.6 %all_to_all.53.rows_ref = f32[32,4,128]{2,1,0:T(4,128)S(1)} all-to-all(f32[32,4,128]{2,1,0:T(4,128)S(1)} %shard_map.70), channel_id=1, replica_groups=mesh['batch'=16,'head'=32] {'head'}, dimensions={0} | all-to-all | bytes 131072 | tf_op jit(solution)/shard_map/all_to_all | solution.py:263
  102.6 22.2 %all_to_all.54.cols_ref = f32[16,16,128]{2,1,0:T(8,128)S(1)} all-to-all(f32[16,16,128]{2,1,0:T(8,128)S(1)} %shard_map.71), channel_id=1, replica_groups=mesh['batch'=16,'head'=32] {'batch'}, dimensions={0} | all-to-all | bytes 262144 | tf_op jit(solution)/shard_map/all_to_all | solution.py:263
  124.8 1.2 shard_map.72
  126.0 17.1 %all_to_all.55.rows_ref = f32[32,8,128]{2,1,0:T(8,128)S(1)} all-to-all(f32[32,8,128]{2,1,0:T(8,128)S(1)} %get-tuple-element.27), channel_id=1, replica_groups=mesh['batch'=16,'head'=32] {'head'}, dimensions={0} | all-to-all | bytes 262144 | tf_op jit(solution)/shard_map/all_to_all | solution.py:263
  143.1 3.3 %shard_map.73 = (f32[4,2,16,2176]{3,2,1,0:T(8,128)S(1)}, f32[4,2,16,2176]{3,2,1,0:T(8,128)S(1)}, f32[4,128,256]{2,1,0:T(8,128)}) custom-call(s32[4]{0:T(128)S(1)} %pad_add_fusion.places_ref, f32[32,8,128]{2,1,0:T(8,128)S(1)} %all_to_all.55.rows_ref, f32[4,128]{1,0:T(4,128)S(1)} %get-tuple-element.28.partition_ref, ...), custom_call_target="tpu_custom_call" | custom-call | tf_op jit(solution)/shard_map/pallas_call | solution.py:26
  146.3 1.9 collective-permute-start
  148.2 2.7 %collective-permute-done = f32[4,2,16,2176]{3,2,1,0:T(8,128)S(1)} collective-permute-done((f32[4,2,16,2176]{3,2,1,0:T(8,128)S(1)}, f32[4,2,16,2176]{3,2,1,0:T(8,128)S(1)}, u32[]{:S(2)}, u32[]{:S(2)}) %collective-permute-start) | collective-permute-done | bytes 1114144 | tf_op jit(solution)/shard_map/ppermute | solution.py:352
  151.1 3.5 %all-to-all-start.6 = ((f32[4,128,256]{2,1,0:T(8,128)}), f32[4,128,256]{2,1,0:T(8,128)S(1)}, u32[]{:S(2)}, u32[]{:S(2)}) async-start(f32[4,128,256]{2,1,0:T(8,128)} %get-tuple-element.37), calls=%async_computation.6 | async-start | bytes 1048576 | tf_op jit(solution)/shard_map/all_to_all | solution.py:263
  154.7 2.4 %collective-permute-start.1 = (f32[2,16,2176]{2,1,0:T(8,128)S(1)}, f32[2,16,2176]{2,1,0:T(8,128)S(1)}, u32[]{:S(2)}, u32[]{:S(2)}) collective-permute-start(f32[2,16,2176]{2,1,0:T(8,128)S(1)} %get-tuple-element.41), channel_id=1, source_target_pairs={{0,128},{32,160},{64,192},{96,224},{128,256},{160,288},{192,320},{... | collective-permute-start | bytes 835592 | tf_op jit(solution)/shard_map/ppermute | solution.py:359
  157.0 4.7 %collective-permute-start.3 = (f32[2,16,2176]{2,1,0:T(8,128)S(1)}, f32[2,16,2176]{2,1,0:T(8,128)S(1)}, u32[]{:S(2)}, u32[]{:S(2)}) collective-permute-start(f32[2,16,2176]{2,1,0:T(8,128)S(1)} %get-tuple-element.42), channel_id=1, source_target_pairs={{0,384},{32,416},{64,448},{96,480},{128,0},{160,32},{192,64},{224,... | collective-permute-start | bytes 835592 | tf_op jit(solution)/shard_map/ppermute | solution.py:359
  161.7 1.9 collective-permute-start.2
  163.7 1.0 all-to-all-done.6
  164.6 0.7 reduce_sum.9
  165.3 5.3 %all-to-all-start.7 = ((f32[8,16,256]{2,1,0:T(8,128)}), f32[8,16,256]{2,1,0:T(8,128)S(1)}, u32[]{:S(2)}, u32[]{:S(2)}) async-start(f32[8,16,256]{2,1,0:T(8,128)} %bitcast.4), calls=%async_computation.7 | async-start | bytes 262144 | tf_op jit(solution)/shard_map/all_to_all | solution.py:263
  170.6 3.1 %collective-permute-done.3 = f32[2,16,2176]{2,1,0:T(8,128)S(1)} collective-permute-done((f32[2,16,2176]{2,1,0:T(8,128)S(1)}, f32[2,16,2176]{2,1,0:T(8,128)S(1)}, u32[]{:S(2)}, u32[]{:S(2)}) %collective-permute-start.3) | collective-permute-done | bytes 278560 | tf_op jit(solution)/shard_map/ppermute | solution.py:359
  173.7 7.5 %all-to-all-done.7.blocks_ref = f32[8,16,256]{2,1,0:T(8,128)S(1)} async-done(((f32[8,16,256]{2,1,0:T(8,128)}), f32[8,16,256]{2,1,0:T(8,128)S(1)}, u32[]{:S(2)}, u32[]{:S(2)}) %all-to-all-start.7) | async-done | bytes 131104 | tf_op jit(solution)/shard_map/all_to_all | solution.py:263
  181.2 0.8 shard_map.74
  182.0 5.1 %all-to-all-start.8 = ((f32[8,16,256]{2,1,0:T(8,128)}), f32[8,16,256]{2,1,0:T(8,128)S(1)}, u32[]{:S(2)}, u32[]{:S(2)}) async-start(f32[8,16,256]{2,1,0:T(8,128)} %shard_map.74), calls=%async_computation.8 | async-start | bytes 262144 | tf_op jit(solution)/shard_map/all_to_all | solution.py:263
  187.1 2.6 %collective-permute-start.4 = (f32[16,2176]{1,0:T(8,128)S(1)}, f32[16,2176]{1,0:T(8,128)S(1)}, u32[]{:S(2)}, u32[]{:S(2)}) collective-permute-start(f32[16,2176]{1,0:T(8,128)S(1)} %slice_bitcast_fusion.3), channel_id=1, source_target_pairs={{0,64},{32,96},{64,0},{96,32},{128,192},{160,224},{192,128},{224,1... | collective-permute-start | bytes 417800 | tf_op jit(solution)/shard_map/ppermute | solution.py:365
  189.6 16.8 %all-to-all-done.8 = f32[8,16,256]{2,1,0:T(8,128)S(1)} async-done(((f32[8,16,256]{2,1,0:T(8,128)}), f32[8,16,256]{2,1,0:T(8,128)S(1)}, u32[]{:S(2)}, u32[]{:S(2)}) %all-to-all-start.8) | async-done | bytes 131104 | tf_op jit(solution)/shard_map/all_to_all | solution.py:263
  206.5 0.8 broadcast_in_dim.8
  207.3 3.8 %all-to-all-start.9 = ((f32[4,128,256]{2,1,0:T(8,128)}), f32[4,128,256]{2,1,0:T(8,128)S(1)}, u32[]{:S(2)}, u32[]{:S(2)}) async-start(f32[4,128,256]{2,1,0:T(8,128)} %broadcast_in_dim.8), calls=%async_computation.9 | async-start | bytes 1048576 | tf_op jit(solution)/shard_map/all_to_all | solution.py:263
  211.6 0.7 slice.34
  213.0 6.2 %all-to-all-done.9 = f32[4,128,256]{2,1,0:T(8,128)S(1)} async-done(((f32[4,128,256]{2,1,0:T(8,128)}), f32[4,128,256]{2,1,0:T(8,128)S(1)}, u32[]{:S(2)}, u32[]{:S(2)}) %all-to-all-start.9) | async-done | bytes 524320 | tf_op jit(solution)/shard_map/all_to_all | solution.py:263
  219.2 0.8 copy.8
  (15 shorter events, 1.9 us)
Async XLA Ops:
  0.7 0.7 copy-start.1
  124.8 18.3 %copy-start = (bf16[256,2048]{1,0:T(8,128)(2,1)S(1)}, bf16[256,2048]{1,0:T(8,128)(2,1)}, u32[]{:S(2)}) copy-start(bf16[256,2048]{1,0:T(8,128)(2,1)} %weight_ref.1) | copy-start | bytes 3145732
  146.3 4.6 %collective-permute-start = (f32[4,2,16,2176]{3,2,1,0:T(8,128)S(1)}, f32[4,2,16,2176]{3,2,1,0:T(8,128)S(1)}, u32[]{:S(2)}, u32[]{:S(2)}) collective-permute-start(f32[4,2,16,2176]{3,2,1,0:T(8,128)S(1)} %get-tuple-element.35), channel_id=1, source_target_pairs={{0,32},{32,0},{64,96},{96,64},{128,160},{160,128},{192,224},{224,1... | collective-permute-start | bytes 3342344 | tf_op jit(solution)/shard_map/ppermute | solution.py:352
  151.1 13.5 %all-to-all-start.6 = ((f32[4,128,256]{2,1,0:T(8,128)}), f32[4,128,256]{2,1,0:T(8,128)S(1)}, u32[]{:S(2)}, u32[]{:S(2)}) async-start(f32[4,128,256]{2,1,0:T(8,128)} %get-tuple-element.37), calls=%async_computation.6 | async-start | bytes 1048576 | tf_op jit(solution)/shard_map/all_to_all | solution.py:263
  154.7 15.9 %collective-permute-start.1 = (f32[2,16,2176]{2,1,0:T(8,128)S(1)}, f32[2,16,2176]{2,1,0:T(8,128)S(1)}, u32[]{:S(2)}, u32[]{:S(2)}) collective-permute-start(f32[2,16,2176]{2,1,0:T(8,128)S(1)} %get-tuple-element.41), channel_id=1, source_target_pairs={{0,128},{32,160},{64,192},{96,224},{128,256},{160,288},{192,320},{... | collective-permute-start | bytes 835592 | tf_op jit(solution)/shard_map/ppermute | solution.py:359
  157.0 16.6 %collective-permute-start.3 = (f32[2,16,2176]{2,1,0:T(8,128)S(1)}, f32[2,16,2176]{2,1,0:T(8,128)S(1)}, u32[]{:S(2)}, u32[]{:S(2)}) collective-permute-start(f32[2,16,2176]{2,1,0:T(8,128)S(1)} %get-tuple-element.42), channel_id=1, source_target_pairs={{0,384},{32,416},{64,448},{96,480},{128,0},{160,32},{192,64},{224,... | collective-permute-start | bytes 835592 | tf_op jit(solution)/shard_map/ppermute | solution.py:359
  161.7 11.9 %collective-permute-start.2 = (f32[2,16,2176]{2,1,0:T(8,128)S(1)}, f32[2,16,2176]{2,1,0:T(8,128)S(1)}, u32[]{:S(2)}, u32[]{:S(2)}) collective-permute-start(f32[2,16,2176]{2,1,0:T(8,128)S(1)} %get-tuple-element.43), channel_id=1, source_target_pairs={{0,256},{32,288},{64,320},{96,352},{128,384},{160,416},{192,448},{... | collective-permute-start | bytes 835592 | tf_op jit(solution)/shard_map/ppermute | solution.py:359
  165.3 15.9 %all-to-all-start.7 = ((f32[8,16,256]{2,1,0:T(8,128)}), f32[8,16,256]{2,1,0:T(8,128)S(1)}, u32[]{:S(2)}, u32[]{:S(2)}) async-start(f32[8,16,256]{2,1,0:T(8,128)} %bitcast.4), calls=%async_computation.7 | async-start | bytes 262144 | tf_op jit(solution)/shard_map/all_to_all | solution.py:263
  182.0 24.5 %all-to-all-start.8 = ((f32[8,16,256]{2,1,0:T(8,128)}), f32[8,16,256]{2,1,0:T(8,128)S(1)}, u32[]{:S(2)}, u32[]{:S(2)}) async-start(f32[8,16,256]{2,1,0:T(8,128)} %shard_map.74), calls=%async_computation.8 | async-start | bytes 262144 | tf_op jit(solution)/shard_map/all_to_all | solution.py:263
  187.1 24.0 %collective-permute-start.4 = (f32[16,2176]{1,0:T(8,128)S(1)}, f32[16,2176]{1,0:T(8,128)S(1)}, u32[]{:S(2)}, u32[]{:S(2)}) collective-permute-start(f32[16,2176]{1,0:T(8,128)S(1)} %slice_bitcast_fusion.3), channel_id=1, source_target_pairs={{0,64},{32,96},{64,0},{96,32},{128,192},{160,224},{192,128},{224,1... | collective-permute-start | bytes 417800 | tf_op jit(solution)/shard_map/ppermute | solution.py:365
  207.3 11.9 %all-to-all-start.9 = ((f32[4,128,256]{2,1,0:T(8,128)}), f32[4,128,256]{2,1,0:T(8,128)S(1)}, u32[]{:S(2)}, u32[]{:S(2)}) async-start(f32[4,128,256]{2,1,0:T(8,128)} %broadcast_in_dim.8), calls=%async_computation.9 | async-start | bytes 1048576 | tf_op jit(solution)/shard_map/all_to_all | solution.py:263

commit v4 on v3

--- a/solution.py
+++ b/solution.py
@@ -10,6 +10,7 @@
 TEACHER_TEMP = 0.07
 STUDENT_TEMP = 0.1
 EPSILON = 1e-06
+LOG2_E = 1.4426950408889634
 LANES = 128
 F32 = jnp.float32
 BF16 = jnp.bfloat16
@@ -90,15 +91,20 @@
 
 
 def start_kernel(
-    places_ref, weight_hbm, teacher_hbm, student_hbm, index_ref,
+    places_ref, weight_hbm, teacher_hbm, student_hbm, index_hbm,
     back_ref, inv_ref, teacher_exp_ref, msg_ref,
     own_unit_ref, own_inv_ref, flip_ref, logits_ref, student_exp_ref, part_ref,
-    weight_ref, teacher_ref, student_ref, norm_ref, unit_ref, row_inv_ref, tail, sems,
+    weight_ref, teacher_ref, student_ref, index_ref, norm_ref, unit_ref, row_inv_ref, tail, sems,
 ):
     copies = [
         pltpu.make_async_copy(source, target, sems.at[i])
         for i, (source, target) in enumerate(
-            [(weight_hbm, weight_ref), (teacher_hbm, teacher_ref), (student_hbm, student_ref)]
+            [
+                (weight_hbm, weight_ref),
+                (index_hbm, index_ref),
+                (teacher_hbm, teacher_ref),
+                (student_hbm, student_ref),
+            ]
         )
     ]
     for copy in copies:
@@ -110,15 +116,16 @@
     norm_ref[...] = (wide * inverse).astype(BF16)
     back_ref[...] = jnp.transpose(norm_ref[...])
     copies[1].wait()
+    copies[2].wait()
     total = jnp.zeros((1, weight_ref.shape[1]), F32)
     for view in range(teacher_ref.shape[0]):
         unit, _ = picked_unit(teacher_ref[view], index_ref[view : view + 1, :])
         logits = jnp.dot(unit.astype(BF16), norm_ref[...], preferred_element_type=F32)
-        block = jnp.exp(logits * (1.0 / TEACHER_TEMP))
+        block = jnp.exp2(logits * (LOG2_E / TEACHER_TEMP))
         teacher_exp_ref[view * LANES : (view + 1) * LANES, :] = block
         total += jnp.sum(block, axis=0, keepdims=True)
-    msg_ref[...] = jnp.broadcast_to(col_tiles(total)[None], msg_ref.shape)
-    copies[2].wait()
+    msg_ref[...] = col_tiles(total)
+    copies[3].wait()
     for view in range(student_ref.shape[0]):
         rows = slice(view * LANES, (view + 1) * LANES)
         unit, inverse = picked_unit(student_ref[view], index_ref[view : view + 1, :])
@@ -127,7 +134,7 @@
         narrow = unit.astype(BF16)
         flip_ref[:, rows] = jnp.transpose(narrow)
         logits = jnp.dot(narrow, norm_ref[...], preferred_element_type=F32)
-        block = jnp.exp(logits * (1.0 / STUDENT_TEMP))
+        block = jnp.exp2(logits * (LOG2_E / STUDENT_TEMP))
         logits_ref[rows, :] = logits
         student_exp_ref[rows, :] = block
         tail[rows, :] = fold(block)
@@ -180,8 +187,7 @@
     sums = lax.fori_loop(
         0, exp_ref.shape[0] // 8, step, (jnp.zeros((8, LANES), F32),) * count, unroll=8
     )
-    total = jnp.concatenate([jnp.sum(s, axis=0, keepdims=True) for s in sums], axis=0)
-    msg_ref[...] = jnp.broadcast_to(total[None], msg_ref.shape)
+    msg_ref[...] = jnp.concatenate([jnp.sum(s, axis=0, keepdims=True) for s in sums], axis=0)
 
 
 def last_row_kernel(cols_ref, exp_ref, logits_ref, msg_ref, scale_ref, tail, weighted):
@@ -251,6 +257,10 @@
                 )
 
 
+def pair_kernel(pair_ref, copies_ref):
+    copies_ref[...] = jnp.broadcast_to(jnp.sum(pair_ref[...], axis=0)[None], copies_ref.shape)
+
+
 def finish_kernel(blocks_ref, unit_ref, inv_ref, copies_ref):
     pull = jnp.sum(blocks_ref[...], axis=0)
     unit = unit_ref[...]
@@ -265,6 +275,14 @@
 
 def share(block, axis, groups, count):
     return exchange(jnp.broadcast_to(block[None], (count,) + block.shape), axis, groups)
+
+
+def over_batch(block):
+    pairs = [[i, i + 1] for i in range(0, 16, 2)]
+    rest = [[i for i in range(16) if i % 2 == core] for core in range(2)]
+    both = lax.all_gather(block, "batch", axis_index_groups=pairs)
+    copies = kernel_call(pair_kernel, shape((8,) + block.shape), limit=4)(both)
+    return exchange(copies, "batch", rest)
 
 
 def tie(*values):
@@ -282,7 +300,7 @@
     places = jnp.stack([batch_index & 1, batch_index >> 2, (batch_index >> 1) & 1, first])
     y_groups = [[4 * z + y for y in range(4)] for z in range(8)]
     z_groups = [[4 * z + y for z in range(8)] for y in range(4)]
-    col_msg = shape((16, columns // LANES, LANES))
+    col_msg = shape((columns // LANES, LANES))
     row_msg = shape((32, total // LANES, LANES))
     row_msg_two = shape((32, 2 * total // LANES, LANES))
     tail = pltpu.VMEM((total, LANES), F32)
@@ -308,19 +326,21 @@
             pltpu.VMEM(weight.shape, BF16),
             pltpu.VMEM(teacher_patches.shape, BF16),
             pltpu.VMEM(student_patches.shape, BF16),
+            pltpu.VMEM(mask_index.shape, jnp.int32),
             pltpu.VMEM((feature_dim, columns), BF16),
             pltpu.VMEM((total, feature_dim), F32),
             tail,
             tail,
-            pltpu.SemaphoreType.DMA((3,)),
+            pltpu.SemaphoreType.DMA((4,)),
         ],
         scalars=1,
-        far=3,
+        far=4,
         limit=16,
     )(
-        places, far_off(weight), far_off(teacher_patches), far_off(student_patches), mask_index
-    )
-    cols = exchange(cols, "batch")
+        places, far_off(weight), far_off(teacher_patches), far_off(student_patches),
+        far_off(mask_index),
+    )
+    cols = over_batch(cols)
     rows = kernel_call(functools.partial(row_kernel, True), row_msg_two, [tail])(
         cols, teacher_exp, partition_part
     )
@@ -328,11 +348,11 @@
     cols, partition = kernel_call(
         functools.partial(col_kernel, True), (col_msg, shape((total // LANES, LANES))), [tail]
     )(rows, teacher_exp)
-    cols = exchange(cols, "batch")
+    cols = over_batch(cols)
     rows = kernel_call(functools.partial(row_kernel, False), row_msg, [tail])(cols, teacher_exp)
     rows = exchange(rows, "head")
     cols = kernel_call(functools.partial(col_kernel, False), col_msg, [tail])(rows, teacher_exp)
-    cols = exchange(cols, "batch")
+    cols = over_batch(cols)
     rows, col_scale = kernel_call(
         last_row_kernel, (row_msg_two, shape((8, columns))), [tail, tail]
     )(cols, teacher_exp, logits)

time: 222 us -> 217 us (0.977)
  the two profiles are of different devices: /device:TPU:32 before, /device:TPU:4 now
where the time goes in v4:
time: 217 us; the launch traced here: 216 us
  blocking collectives  129 us (59%)
  waiting for transfers between devices  36.7 us (17%)
  starting transfers between devices  31.4 us (14%)
  Pallas kernels  13.3 us (6%)
  local copies, waits for them, and re-layouts  2.87 us (1%)
  between operations  2.57 us (1%)
    all_to_all x6, blocking collectives, exchange(): return lax.all_to_all(blocks, axis, 0, 0, axis_index_groups=groups)  123 us
    all_to_all x4, waiting for transfers between devices, exchange(): return lax.all_to_all(blocks, axis, 0, 0, axis_index_groups=groups)  32.2 us
    all_to_all x4, starting transfers between devices, exchange(): return lax.all_to_all(blocks, axis, 0, 0, axis_index_groups=groups)  15.9 us
    pallas_call x11, Pallas kernels, call(): pl.pallas_call(body, out_shape=out_shape, in_specs=specs, out_specs=jax.t...  13.3 us
    ppermute x3, starting transfers between devices, per_device(): held = held + lax.ppermute(parts[step], 'batch', pairs)  11.3 us
    all_gather x3, blocking collectives, over_batch(): both = lax.all_gather(block, 'batch', axis_index_groups=pairs)  5.44 us
  transfers between devices with their start and end apart: 9, of which 5 were waited for; matrix products, arithmetic and copies ran while one was open for 1% of the time, Pallas kernels for 0%

profile of v4, /device:TPU:4, one launch (start us, length us, event | category | flops | bytes accessed | tf_op | source)
XLA Modules:
  0.0 216.4 jit_solution(15040630525741154033)
XLA Ops:
  0.7 5.9 %shard_map.67 = (bf16[2048,256]{1,0:T(8,128)(2,1)S(1)}, f32[1,2048]{1,0:T(1,128)S(1)}, f32[512,2048]{1,0:T(8,128)S(1)}, f32[16,128]{1,0:T(8,128)S(1)}, f32[16,25...) custom-call(s32[4]{0:T(128)S(1)} %pad_add_fusion.places_ref, ...), custom_call_target="tpu_custom_call" | custom-call | tf_op jit(solution)/shard_map/pallas_call | solution.py:27
  6.6 1.8 all-gather
  8.4 30.6 %all_to_all.50.refs_0_ = f32[8,16,128]{2,1,0:T(8,128)S(1)} all-to-all(f32[8,16,128]{2,1,0:T(8,128)S(1)} %shard_map.68), channel_id=1, replica_groups={{0,64,128,192,256,320,384,448},{32,96,160,224,288,352,416,480},{1,65,12..., dimensions={0} | all-to-all | bytes 131072 | tf_op jit(solution)/shard_map/all_to_all | solution.py:273
  39.1 0.6 shard_map.69
  39.7 21.4 %all_to_all.51.rows_ref = f32[32,8,128]{2,1,0:T(8,128)S(1)} all-to-all(f32[32,8,128]{2,1,0:T(8,128)S(1)} %shard_map.69), channel_id=1, replica_groups=mesh['batch'=16,'head'=32] {'head'}, dimensions={0} | all-to-all | bytes 262144 | tf_op jit(solution)/shard_map/all_to_all | solution.py:273
  61.6 1.8 all-gather.1
  63.5 17.5 %all_to_all.52.refs_0_ = f32[8,16,128]{2,1,0:T(8,128)S(1)} all-to-all(f32[8,16,128]{2,1,0:T(8,128)S(1)} %shard_map.71), channel_id=1, replica_groups={{0,64,128,192,256,320,384,448},{32,96,160,224,288,352,416,480},{1,65,12..., dimensions={0} | all-to-all | bytes 131072 | tf_op jit(solution)/shard_map/all_to_all | solution.py:273
  81.6 17.6 %all_to_all.53.rows_ref = f32[32,4,128]{2,1,0:T(4,128)S(1)} all-to-all(f32[32,4,128]{2,1,0:T(4,128)S(1)} %shard_map.72), channel_id=1, replica_groups=mesh['batch'=16,'head'=32] {'head'}, dimensions={0} | all-to-all | bytes 131072 | tf_op jit(solution)/shard_map/all_to_all | solution.py:273
  99.7 1.8 all-gather.2
  101.5 17.5 %all_to_all.54.cols_ref = f32[8,16,128]{2,1,0:T(8,128)S(1)} all-to-all(f32[8,16,128]{2,1,0:T(8,128)S(1)} %shard_map.74), channel_id=1, replica_groups={{0,64,128,192,256,320,384,448},{32,96,160,224,288,352,416,480},{1,65,12..., dimensions={0} | all-to-all | bytes 131072 | tf_op jit(solution)/shard_map/all_to_all | solution.py:273
  119.0 1.2 shard_map.75
  120.2 18.5 %all_to_all.55.rows_ref = f32[32,8,128]{2,1,0:T(8,128)S(1)} all-to-all(f32[32,8,128]{2,1,0:T(8,128)S(1)} %get-tuple-element.27), channel_id=1, replica_groups=mesh['batch'=16,'head'=32] {'head'}, dimensions={0} | all-to-all | bytes 262144 | tf_op jit(solution)/shard_map/all_to_all | solution.py:273
  138.7 3.1 %shard_map.76 = (f32[4,2,16,2176]{3,2,1,0:T(8,128)S(1)}, f32[4,2,16,2176]{3,2,1,0:T(8,128)S(1)}, f32[4,128,256]{2,1,0:T(8,128)}) custom-call(s32[4]{0:T(128)S(1)} %pad_add_fusion.places_ref, f32[32,8,128]{2,1,0:T(8,128)S(1)} %all_to_all.55.rows_ref, f32[4,128]{1,0:T(4,128)S(1)} %get-tuple-element.28.partition_ref, ...), custom_call_target="tpu_custom_call" | custom-call | tf_op jit(solution)/shard_map/pallas_call | solution.py:27
  141.8 1.9 collective-permute-start
  143.7 2.7 %collective-permute-done = f32[4,2,16,2176]{3,2,1,0:T(8,128)S(1)} collective-permute-done((f32[4,2,16,2176]{3,2,1,0:T(8,128)S(1)}, f32[4,2,16,2176]{3,2,1,0:T(8,128)S(1)}, u32[]{:S(2)}, u32[]{:S(2)}) %collective-permute-start) | collective-permute-done | bytes 1114144 | tf_op jit(solution)/shard_map/ppermute | solution.py:372
  146.6 3.5 %all-to-all-start.6 = ((f32[4,128,256]{2,1,0:T(8,128)}), f32[4,128,256]{2,1,0:T(8,128)S(1)}, u32[]{:S(2)}, u32[]{:S(2)}) async-start(f32[4,128,256]{2,1,0:T(8,128)} %get-tuple-element.37), calls=%async_computation.6 | async-start | bytes 1048576 | tf_op jit(solution)/shard_map/all_to_all | solution.py:273
  150.2 3.2 %collective-permute-start.1 = (f32[2,16,2176]{2,1,0:T(8,128)S(1)}, f32[2,16,2176]{2,1,0:T(8,128)S(1)}, u32[]{:S(2)}, u32[]{:S(2)}) collective-permute-start(f32[2,16,2176]{2,1,0:T(8,128)S(1)} %get-tuple-element.41), channel_id=1, source_target_pairs={{0,128},{32,160},{64,192},{96,224},{128,256},{160,288},{192,320},{... | collective-permute-start | bytes 835592 | tf_op jit(solution)/shard_map/ppermute | solution.py:379
  153.4 2.6 %collective-permute-start.3 = (f32[2,16,2176]{2,1,0:T(8,128)S(1)}, f32[2,16,2176]{2,1,0:T(8,128)S(1)}, u32[]{:S(2)}, u32[]{:S(2)}) collective-permute-start(f32[2,16,2176]{2,1,0:T(8,128)S(1)} %get-tuple-element.42), channel_id=1, source_target_pairs={{0,384},{32,416},{64,448},{96,480},{128,0},{160,32},{192,64},{224,... | collective-permute-start | bytes 835592 | tf_op jit(solution)/shard_map/ppermute | solution.py:379
  156.0 5.5 %collective-permute-start.2 = (f32[2,16,2176]{2,1,0:T(8,128)S(1)}, f32[2,16,2176]{2,1,0:T(8,128)S(1)}, u32[]{:S(2)}, u32[]{:S(2)}) collective-permute-start(f32[2,16,2176]{2,1,0:T(8,128)S(1)} %get-tuple-element.43), channel_id=1, source_target_pairs={{0,256},{32,288},{64,320},{96,352},{128,384},{160,416},{192,448},{... | collective-permute-start | bytes 835592 | tf_op jit(solution)/shard_map/ppermute | solution.py:379
  161.5 0.7 reduce_sum.9
  162.2 3.8 %all-to-all-start.7 = ((f32[8,16,256]{2,1,0:T(8,128)}), f32[8,16,256]{2,1,0:T(8,128)S(1)}, u32[]{:S(2)}, u32[]{:S(2)}) async-start(f32[8,16,256]{2,1,0:T(8,128)} %bitcast.7), calls=%async_computation.7 | async-start | bytes 262144 | tf_op jit(solution)/shard_map/all_to_all | solution.py:273
  166.0 1.9 collective-permute-done.2
  167.9 9.6 %all-to-all-done.7.blocks_ref = f32[8,16,256]{2,1,0:T(8,128)S(1)} async-done(((f32[8,16,256]{2,1,0:T(8,128)}), f32[8,16,256]{2,1,0:T(8,128)S(1)}, u32[]{:S(2)}, u32[]{:S(2)}) %all-to-all-start.7) | async-done | bytes 131104 | tf_op jit(solution)/shard_map/all_to_all | solution.py:273
  177.5 0.8 shard_map.77
  178.3 4.2 %all-to-all-start.8 = ((f32[8,16,256]{2,1,0:T(8,128)}), f32[8,16,256]{2,1,0:T(8,128)S(1)}, u32[]{:S(2)}, u32[]{:S(2)}) async-start(f32[8,16,256]{2,1,0:T(8,128)} %shard_map.77), calls=%async_computation.8 | async-start | bytes 262144 | tf_op jit(solution)/shard_map/all_to_all | solution.py:273
  182.5 2.3 %collective-permute-start.4 = (f32[16,2176]{1,0:T(8,128)S(1)}, f32[16,2176]{1,0:T(8,128)S(1)}, u32[]{:S(2)}, u32[]{:S(2)}) collective-permute-start(f32[16,2176]{1,0:T(8,128)S(1)} %slice_bitcast_fusion.3), channel_id=1, source_target_pairs={{0,64},{32,96},{64,0},{96,32},{128,192},{160,224},{192,128},{224,1... | collective-permute-start | bytes 417800 | tf_op jit(solution)/shard_map/ppermute | solution.py:385
  184.8 16.3 %all-to-all-done.8 = f32[8,16,256]{2,1,0:T(8,128)S(1)} async-done(((f32[8,16,256]{2,1,0:T(8,128)}), f32[8,16,256]{2,1,0:T(8,128)S(1)}, u32[]{:S(2)}, u32[]{:S(2)}) %all-to-all-start.8) | async-done | bytes 131104 | tf_op jit(solution)/shard_map/all_to_all | solution.py:273
  201.1 0.8 broadcast_in_dim.8
  201.9 4.5 %all-to-all-start.9 = ((f32[4,128,256]{2,1,0:T(8,128)}), f32[4,128,256]{2,1,0:T(8,128)S(1)}, u32[]{:S(2)}, u32[]{:S(2)}) async-start(f32[4,128,256]{2,1,0:T(8,128)} %broadcast_in_dim.8), calls=%async_computation.9 | async-start | bytes 1048576 | tf_op jit(solution)/shard_map/all_to_all | solution.py:273
  207.0 0.7 slice.34
  208.3 6.2 %all-to-all-done.9 = f32[4,128,256]{2,1,0:T(8,128)S(1)} async-done(((f32[4,128,256]{2,1,0:T(8,128)}), f32[4,128,256]{2,1,0:T(8,128)S(1)}, u32[]{:S(2)}, u32[]{:S(2)}) %all-to-all-start.9) | async-done | bytes 524320 | tf_op jit(solution)/shard_map/all_to_all | solution.py:273
  214.5 0.8 copy.8
  (19 shorter events, 2.6 us)
Async XLA Ops:
  119.0 19.7 %copy-start = (bf16[256,2048]{1,0:T(8,128)(2,1)S(1)}, bf16[256,2048]{1,0:T(8,128)(2,1)}, u32[]{:S(2)}) copy-start(bf16[256,2048]{1,0:T(8,128)(2,1)} %weight_ref.1) | copy-start | bytes 3145732
  141.8 4.6 %collective-permute-start = (f32[4,2,16,2176]{3,2,1,0:T(8,128)S(1)}, f32[4,2,16,2176]{3,2,1,0:T(8,128)S(1)}, u32[]{:S(2)}, u32[]{:S(2)}) collective-permute-start(f32[4,2,16,2176]{3,2,1,0:T(8,128)S(1)} %get-tuple-element.35), channel_id=1, source_target_pairs={{0,32},{32,0},{64,96},{96,64},{128,160},{160,128},{192,224},{224,1... | collective-permute-start | bytes 3342344 | tf_op jit(solution)/shard_map/ppermute | solution.py:372
  146.6 14.9 %all-to-all-start.6 = ((f32[4,128,256]{2,1,0:T(8,128)}), f32[4,128,256]{2,1,0:T(8,128)S(1)}, u32[]{:S(2)}, u32[]{:S(2)}) async-start(f32[4,128,256]{2,1,0:T(8,128)} %get-tuple-element.37), calls=%async_computation.6 | async-start | bytes 1048576 | tf_op jit(solution)/shard_map/all_to_all | solution.py:273
  150.2 15.8 %collective-permute-start.1 = (f32[2,16,2176]{2,1,0:T(8,128)S(1)}, f32[2,16,2176]{2,1,0:T(8,128)S(1)}, u32[]{:S(2)}, u32[]{:S(2)}) collective-permute-start(f32[2,16,2176]{2,1,0:T(8,128)S(1)} %get-tuple-element.41), channel_id=1, source_target_pairs={{0,128},{32,160},{64,192},{96,224},{128,256},{160,288},{192,320},{... | collective-permute-start | bytes 835592 | tf_op jit(solution)/shard_map/ppermute | solution.py:379
  153.4 12.6 %collective-permute-start.3 = (f32[2,16,2176]{2,1,0:T(8,128)S(1)}, f32[2,16,2176]{2,1,0:T(8,128)S(1)}, u32[]{:S(2)}, u32[]{:S(2)}) collective-permute-start(f32[2,16,2176]{2,1,0:T(8,128)S(1)} %get-tuple-element.42), channel_id=1, source_target_pairs={{0,384},{32,416},{64,448},{96,480},{128,0},{160,32},{192,64},{224,... | collective-permute-start | bytes 835592 | tf_op jit(solution)/shard_map/ppermute | solution.py:379
  156.0 11.9 %collective-permute-start.2 = (f32[2,16,2176]{2,1,0:T(8,128)S(1)}, f32[2,16,2176]{2,1,0:T(8,128)S(1)}, u32[]{:S(2)}, u32[]{:S(2)}) collective-permute-start(f32[2,16,2176]{2,1,0:T(8,128)S(1)} %get-tuple-element.43), channel_id=1, source_target_pairs={{0,256},{32,288},{64,320},{96,352},{128,384},{160,416},{192,448},{... | collective-permute-start | bytes 835592 | tf_op jit(solution)/shard_map/ppermute | solution.py:379
  162.2 15.3 %all-to-all-start.7 = ((f32[8,16,256]{2,1,0:T(8,128)}), f32[8,16,256]{2,1,0:T(8,128)S(1)}, u32[]{:S(2)}, u32[]{:S(2)}) async-start(f32[8,16,256]{2,1,0:T(8,128)} %bitcast.7), calls=%async_computation.7 | async-start | bytes 262144 | tf_op jit(solution)/shard_map/all_to_all | solution.py:273
  178.3 22.8 %all-to-all-start.8 = ((f32[8,16,256]{2,1,0:T(8,128)}), f32[8,16,256]{2,1,0:T(8,128)S(1)}, u32[]{:S(2)}, u32[]{:S(2)}) async-start(f32[8,16,256]{2,1,0:T(8,128)} %shard_map.77), calls=%async_computation.8 | async-start | bytes 262144 | tf_op jit(solution)/shard_map/all_to_all | solution.py:273
  182.5 24.0 %collective-permute-start.4 = (f32[16,2176]{1,0:T(8,128)S(1)}, f32[16,2176]{1,0:T(8,128)S(1)}, u32[]{:S(2)}, u32[]{:S(2)}) collective-permute-start(f32[16,2176]{1,0:T(8,128)S(1)} %slice_bitcast_fusion.3), channel_id=1, source_target_pairs={{0,64},{32,96},{64,0},{96,32},{128,192},{160,224},{192,128},{224,1... | collective-permute-start | bytes 417800 | tf_op jit(solution)/shard_map/ppermute | solution.py:385
  201.9 12.6 %all-to-all-start.9 = ((f32[4,128,256]{2,1,0:T(8,128)}), f32[4,128,256]{2,1,0:T(8,128)S(1)}, u32[]{:S(2)}, u32[]{:S(2)}) async-start(f32[4,128,256]{2,1,0:T(8,128)} %broadcast_in_dim.8), calls=%async_computation.9 | async-start | bytes 1048576 | tf_op jit(solution)/shard_map/all_to_all | solution.py:273

commit v5 on v4

--- a/solution.py
+++ b/solution.py
@@ -91,18 +91,19 @@
 
 
 def start_kernel(
-    places_ref, weight_hbm, teacher_hbm, student_hbm, index_hbm,
+    weight_hbm, teacher_hbm, student_hbm, index_hbm,
     back_ref, inv_ref, teacher_exp_ref, msg_ref,
     own_unit_ref, own_inv_ref, flip_ref, logits_ref, student_exp_ref, part_ref,
-    weight_ref, teacher_ref, student_ref, index_ref, norm_ref, unit_ref, row_inv_ref, tail, sems,
+    weight_ref, teacher_ref, student_ref, index_ref, norm_ref, teacher_norm_ref, unit_ref, row_inv_ref,
+    tail, sems,
 ):
     copies = [
         pltpu.make_async_copy(source, target, sems.at[i])
         for i, (source, target) in enumerate(
             [
-                (weight_hbm, weight_ref),
                 (index_hbm, index_ref),
                 (teacher_hbm, teacher_ref),
+                (weight_hbm, weight_ref),
                 (student_hbm, student_ref),
             ]
         )
@@ -110,19 +111,22 @@
     for copy in copies:
         copy.start()
     copies[0].wait()
+    copies[1].wait()
+    for view in range(teacher_ref.shape[0]):
+        unit, _ = picked_unit(teacher_ref[view], index_ref[view : view + 1, :])
+        teacher_norm_ref[view * LANES : (view + 1) * LANES, :] = unit.astype(BF16)
+    copies[2].wait()
     wide = weight_ref[...].astype(F32)
     inverse = lax.rsqrt(jnp.sum(wide * wide, axis=0, keepdims=True) + EPSILON)
     inv_ref[...] = inverse
     norm_ref[...] = (wide * inverse).astype(BF16)
     back_ref[...] = jnp.transpose(norm_ref[...])
-    copies[1].wait()
-    copies[2].wait()
     total = jnp.zeros((1, weight_ref.shape[1]), F32)
     for view in range(teacher_ref.shape[0]):
-        unit, _ = picked_unit(teacher_ref[view], index_ref[view : view + 1, :])
-        logits = jnp.dot(unit.astype(BF16), norm_ref[...], preferred_element_type=F32)
+        rows = slice(view * LANES, (view + 1) * LANES)
+        logits = jnp.dot(teacher_norm_ref[rows, :], norm_ref[...], preferred_element_type=F32)
         block = jnp.exp2(logits * (LOG2_E / TEACHER_TEMP))
-        teacher_exp_ref[view * LANES : (view + 1) * LANES, :] = block
+        teacher_exp_ref[rows, :] = block
         total += jnp.sum(block, axis=0, keepdims=True)
     msg_ref[...] = col_tiles(total)
     copies[3].wait()
@@ -139,7 +143,9 @@
         student_exp_ref[rows, :] = block
         tail[rows, :] = fold(block)
     part_ref[...] = row_sums(tail[...])
-    own = pl.ds(pl.multiple_of(places_ref[3], 16), own_unit_ref.shape[0])
+    head_index = lax.axis_index("head")
+    first = (head_index & 3) * LANES + (head_index >> 2) * own_unit_ref.shape[0]
+    own = pl.ds(pl.multiple_of(first, 16), own_unit_ref.shape[0])
     own_unit_ref[...] = unit_ref[own, :]
     own_inv_ref[...] = row_inv_ref[own, :]
 
@@ -208,7 +214,7 @@
 
 
 def grad_kernel(
-    places_ref, rows_ref, partition_ref, scale_ref, exp_ref, student_ref, flip_ref, back_ref,
+    rows_ref, partition_ref, scale_ref, exp_ref, student_ref, flip_ref, back_ref,
     weight_ref, inv_ref, keep_ref, send_ref, pull_ref, factor, softener, logits,
 ):
     total = jnp.sum(rows_ref[...], axis=0)
@@ -225,7 +231,8 @@
         factor[rows, :] = column(scale[j : j + 1, :])
         softener[rows, :] = column(softener_rows[j : j + 1, :])
     width = logits.shape[1]
-    core, x_index, z_high = places_ref[0], places_ref[1], places_ref[2]
+    batch_index = lax.axis_index("batch")
+    core, x_index, z_high = batch_index & 1, batch_index >> 2, (batch_index >> 1) & 1
     wide = (LANES, width)
     for block in range(columns // width):
         cols = slice(block * width, (block + 1) * width)
@@ -294,10 +301,6 @@
     feature_dim, columns = weight.shape
     total = view_count * masked_count
     share_rows = feature_dim // 16
-    batch_index = lax.axis_index("batch")
-    head_index = lax.axis_index("head")
-    first = (head_index & 3) * (total // 4) + (head_index >> 2) * (total // 32)
-    places = jnp.stack([batch_index & 1, batch_index >> 2, (batch_index >> 1) & 1, first])
     y_groups = [[4 * z + y for y in range(4)] for z in range(8)]
     z_groups = [[4 * z + y for z in range(8)] for y in range(4)]
     col_msg = shape((columns // LANES, LANES))
@@ -328,16 +331,16 @@
             pltpu.VMEM(student_patches.shape, BF16),
             pltpu.VMEM(mask_index.shape, jnp.int32),
             pltpu.VMEM((feature_dim, columns), BF16),
+            pltpu.VMEM((total, feature_dim), BF16),
             pltpu.VMEM((total, feature_dim), F32),
             tail,
             tail,
             pltpu.SemaphoreType.DMA((4,)),
         ],
-        scalars=1,
         far=4,
         limit=16,
     )(
-        places, far_off(weight), far_off(teacher_patches), far_off(student_patches),
+        far_off(weight), far_off(teacher_patches), far_off(student_patches),
         far_off(mask_index),
     )
     cols = over_batch(cols)
@@ -363,10 +366,9 @@
         grad_kernel,
         (part, part, shape((4, total // 4, feature_dim))),
         [tail, tail, pltpu.VMEM((total, 512), BF16)],
-        scalars=1,
         limit=16,
     )(
-        places, rows, partition, col_scale, teacher_exp, student_exp, flip, back, weight,
+        rows, partition, col_scale, teacher_exp, student_exp, flip, back, weight,
         weight_inv,
     )
     parts = keep + lax.ppermute(send, "batch", [(i, i ^ 1) for i in range(16)])

time: 217 us -> 215 us (level)
  no operation moved by 1% of the time
where the time goes in v5:
time: 215 us
  blocking collectives  129 us (60%)
  waiting for transfers between devices  36.8 us (17%)
  starting transfers between devices  31.4 us (15%)
  Pallas kernels  11.6 us (5%)
  local copies, waits for them, and re-layouts  2.87 us (1%)
  between operations  2.56 us (1%)
    all_to_all x6, blocking collectives, exchange(): return lax.all_to_all(blocks, axis, 0, 0, axis_index_groups=groups)  123 us
    all_to_all x4, waiting for transfers between devices, exchange(): return lax.all_to_all(blocks, axis, 0, 0, axis_index_groups=groups)  32.2 us
    all_to_all x4, starting transfers between devices, exchange(): return lax.all_to_all(blocks, axis, 0, 0, axis_index_groups=groups)  15.9 us
    pallas_call x11, Pallas kernels, call(): pl.pallas_call(body, out_shape=out_shape, in_specs=specs, out_specs=jax.t...  11.6 us
    ppermute x3, starting transfers between devices, per_device(): held = held + lax.ppermute(parts[step], 'batch', pairs)  11.3 us
    all_gather x3, blocking collectives, over_batch(): both = lax.all_gather(block, 'batch', axis_index_groups=pairs)  5.44 us
  transfers between devices with their start and end apart: 9, of which 5 were waited for; matrix products, arithmetic and copies ran while one was open for 1% of the time, Pallas kernels for 0%

profile of v5, /device:TPU:4, one launch (start us, length us, event | category | flops | bytes accessed | tf_op | source)
XLA Modules:
  0.0 214.6 jit_solution(12219051407018351000)
XLA Ops:
  0.6 4.6 %shard_map.67 = (bf16[2048,256]{1,0:T(8,128)(2,1)S(1)}, f32[1,2048]{1,0:T(1,128)S(1)}, f32[512,2048]{1,0:T(8,128)S(1)}, f32[16,128]{1,0:T(8,128)S(1)}, f32[16,25...) custom-call(bf16[256,2048]{1,0:T(8,128)(2,1)} %weight_ref.1, ...), custom_call_target="tpu_custom_call" | custom-call | tf_op jit(solution)/shard_map/pallas_call | solution.py:27
  5.2 1.8 all-gather
  7.0 30.6 %all_to_all.50.refs_0_ = f32[8,16,128]{2,1,0:T(8,128)S(1)} all-to-all(f32[8,16,128]{2,1,0:T(8,128)S(1)} %shard_map.68), channel_id=1, replica_groups={{0,64,128,192,256,320,384,448},{32,96,160,224,288,352,416,480},{1,65,12..., dimensions={0} | all-to-all | bytes 131072 | tf_op jit(solution)/shard_map/all_to_all | solution.py:280
  37.7 0.6 shard_map.69
  38.3 21.4 %all_to_all.51.rows_ref = f32[32,8,128]{2,1,0:T(8,128)S(1)} all-to-all(f32[32,8,128]{2,1,0:T(8,128)S(1)} %shard_map.69), channel_id=1, replica_groups=mesh['batch'=16,'head'=32] {'head'}, dimensions={0} | all-to-all | bytes 262144 | tf_op jit(solution)/shard_map/all_to_all | solution.py:280
  60.2 1.8 all-gather.1
  62.1 17.5 %all_to_all.52.refs_0_ = f32[8,16,128]{2,1,0:T(8,128)S(1)} all-to-all(f32[8,16,128]{2,1,0:T(8,128)S(1)} %shard_map.71), channel_id=1, replica_groups={{0,64,128,192,256,320,384,448},{32,96,160,224,288,352,416,480},{1,65,12..., dimensions={0} | all-to-all | bytes 131072 | tf_op jit(solution)/shard_map/all_to_all | solution.py:280
  80.2 17.6 %all_to_all.53.rows_ref = f32[32,4,128]{2,1,0:T(4,128)S(1)} all-to-all(f32[32,4,128]{2,1,0:T(4,128)S(1)} %shard_map.72), channel_id=1, replica_groups=mesh['batch'=16,'head'=32] {'head'}, dimensions={0} | all-to-all | bytes 131072 | tf_op jit(solution)/shard_map/all_to_all | solution.py:280
  98.3 1.8 all-gather.2
  100.1 17.5 %all_to_all.54.cols_ref = f32[8,16,128]{2,1,0:T(8,128)S(1)} all-to-all(f32[8,16,128]{2,1,0:T(8,128)S(1)} %shard_map.74), channel_id=1, replica_groups={{0,64,128,192,256,320,384,448},{32,96,160,224,288,352,416,480},{1,65,12..., dimensions={0} | all-to-all | bytes 131072 | tf_op jit(solution)/shard_map/all_to_all | solution.py:280
  117.6 1.2 shard_map.75
  118.8 18.5 %all_to_all.55.rows_ref = f32[32,8,128]{2,1,0:T(8,128)S(1)} all-to-all(f32[32,8,128]{2,1,0:T(8,128)S(1)} %get-tuple-element.27), channel_id=1, replica_groups=mesh['batch'=16,'head'=32] {'head'}, dimensions={0} | all-to-all | bytes 262144 | tf_op jit(solution)/shard_map/all_to_all | solution.py:280
  137.3 2.7 %shard_map.76 = (f32[4,2,16,2176]{3,2,1,0:T(8,128)S(1)}, f32[4,2,16,2176]{3,2,1,0:T(8,128)S(1)}, f32[4,128,256]{2,1,0:T(8,128)}) custom-call(f32[32,8,128]{2,1,0:T(8,128)S(1)} %all_to_all.55.rows_ref, f32[4,128]{1,0:T(4,128)S(1)} %get-tuple-element.28.partition_ref, f32[8,2048]{1,0:T(8,128)S(1)} %get-tuple-element.29.scale_ref, ...), custom_call_target="tpu_custom_call" | custom-call | tf_op jit(solution)/shard_map/pallas_call | solution.py:27
  140.0 1.9 collective-permute-start
  142.0 2.7 %collective-permute-done = f32[4,2,16,2176]{3,2,1,0:T(8,128)S(1)} collective-permute-done((f32[4,2,16,2176]{3,2,1,0:T(8,128)S(1)}, f32[4,2,16,2176]{3,2,1,0:T(8,128)S(1)}, u32[]{:S(2)}, u32[]{:S(2)}) %collective-permute-start) | collective-permute-done | bytes 1114144 | tf_op jit(solution)/shard_map/ppermute | solution.py:374
  144.8 3.5 %all-to-all-start.6 = ((f32[4,128,256]{2,1,0:T(8,128)}), f32[4,128,256]{2,1,0:T(8,128)S(1)}, u32[]{:S(2)}, u32[]{:S(2)}) async-start(f32[4,128,256]{2,1,0:T(8,128)} %get-tuple-element.37), calls=%async_computation.6 | async-start | bytes 1048576 | tf_op jit(solution)/shard_map/all_to_all | solution.py:280
  148.3 3.2 %collective-permute-start.1 = (f32[2,16,2176]{2,1,0:T(8,128)S(1)}, f32[2,16,2176]{2,1,0:T(8,128)S(1)}, u32[]{:S(2)}, u32[]{:S(2)}) collective-permute-start(f32[2,16,2176]{2,1,0:T(8,128)S(1)} %get-tuple-element.41), channel_id=1, source_target_pairs={{0,128},{32,160},{64,192},{96,224},{128,256},{160,288},{192,320},{... | collective-permute-start | bytes 835592 | tf_op jit(solution)/shard_map/ppermute | solution.py:381
  151.6 2.6 %collective-permute-start.3 = (f32[2,16,2176]{2,1,0:T(8,128)S(1)}, f32[2,16,2176]{2,1,0:T(8,128)S(1)}, u32[]{:S(2)}, u32[]{:S(2)}) collective-permute-start(f32[2,16,2176]{2,1,0:T(8,128)S(1)} %get-tuple-element.42), channel_id=1, source_target_pairs={{0,384},{32,416},{64,448},{96,480},{128,0},{160,32},{192,64},{224,... | collective-permute-start | bytes 835592 | tf_op jit(solution)/shard_map/ppermute | solution.py:381
  154.2 5.5 %collective-permute-start.2 = (f32[2,16,2176]{2,1,0:T(8,128)S(1)}, f32[2,16,2176]{2,1,0:T(8,128)S(1)}, u32[]{:S(2)}, u32[]{:S(2)}) collective-permute-start(f32[2,16,2176]{2,1,0:T(8,128)S(1)} %get-tuple-element.43), channel_id=1, source_target_pairs={{0,256},{32,288},{64,320},{96,352},{128,384},{160,416},{192,448},{... | collective-permute-start | bytes 835592 | tf_op jit(solution)/shard_map/ppermute | solution.py:381
  159.7 0.7 reduce_sum.9
  160.4 3.8 %all-to-all-start.7 = ((f32[8,16,256]{2,1,0:T(8,128)}), f32[8,16,256]{2,1,0:T(8,128)S(1)}, u32[]{:S(2)}, u32[]{:S(2)}) async-start(f32[8,16,256]{2,1,0:T(8,128)} %bitcast.3), calls=%async_computation.7 | async-start | bytes 262144 | tf_op jit(solution)/shard_map/all_to_all | solution.py:280
  164.2 1.9 collective-permute-done.2
  166.1 9.6 %all-to-all-done.7.blocks_ref = f32[8,16,256]{2,1,0:T(8,128)S(1)} async-done(((f32[8,16,256]{2,1,0:T(8,128)}), f32[8,16,256]{2,1,0:T(8,128)S(1)}, u32[]{:S(2)}, u32[]{:S(2)}) %all-to-all-start.7) | async-done | bytes 131104 | tf_op jit(solution)/shard_map/all_to_all | solution.py:280
  175.7 0.8 shard_map.77
  176.5 4.2 %all-to-all-start.8 = ((f32[8,16,256]{2,1,0:T(8,128)}), f32[8,16,256]{2,1,0:T(8,128)S(1)}, u32[]{:S(2)}, u32[]{:S(2)}) async-start(f32[8,16,256]{2,1,0:T(8,128)} %shard_map.77), calls=%async_computation.8 | async-start | bytes 262144 | tf_op jit(solution)/shard_map/all_to_all | solution.py:280
  180.7 2.3 %collective-permute-start.4 = (f32[16,2176]{1,0:T(8,128)S(1)}, f32[16,2176]{1,0:T(8,128)S(1)}, u32[]{:S(2)}, u32[]{:S(2)}) collective-permute-start(f32[16,2176]{1,0:T(8,128)S(1)} %slice_bitcast_fusion.3), channel_id=1, source_target_pairs={{0,64},{32,96},{64,0},{96,32},{128,192},{160,224},{192,128},{224,1... | collective-permute-start | bytes 417800 | tf_op jit(solution)/shard_map/ppermute | solution.py:387
  182.9 16.3 %all-to-all-done.8 = f32[8,16,256]{2,1,0:T(8,128)S(1)} async-done(((f32[8,16,256]{2,1,0:T(8,128)}), f32[8,16,256]{2,1,0:T(8,128)S(1)}, u32[]{:S(2)}, u32[]{:S(2)}) %all-to-all-start.8) | async-done | bytes 131104 | tf_op jit(solution)/shard_map/all_to_all | solution.py:280
  199.3 0.8 broadcast_in_dim.8
  200.1 4.5 %all-to-all-start.9 = ((f32[4,128,256]{2,1,0:T(8,128)}), f32[4,128,256]{2,1,0:T(8,128)S(1)}, u32[]{:S(2)}, u32[]{:S(2)}) async-start(f32[4,128,256]{2,1,0:T(8,128)} %broadcast_in_dim.8), calls=%async_computation.9 | async-start | bytes 1048576 | tf_op jit(solution)/shard_map/all_to_all | solution.py:280
  205.1 0.7 slice.34
  206.5 6.2 %all-to-all-done.9 = f32[4,128,256]{2,1,0:T(8,128)S(1)} async-done(((f32[4,128,256]{2,1,0:T(8,128)}), f32[4,128,256]{2,1,0:T(8,128)S(1)}, u32[]{:S(2)}, u32[]{:S(2)}) %all-to-all-start.9) | async-done | bytes 524320 | tf_op jit(solution)/shard_map/all_to_all | solution.py:280
  212.7 0.8 copy.8
  (18 shorter events, 2.5 us)
Async XLA Ops:
  117.6 19.7 %copy-start = (bf16[256,2048]{1,0:T(8,128)(2,1)S(1)}, bf16[256,2048]{1,0:T(8,128)(2,1)}, u32[]{:S(2)}) copy-start(bf16[256,2048]{1,0:T(8,128)(2,1)} %weight_ref.1) | copy-start | bytes 3145732
  140.0 4.6 %collective-permute-start = (f32[4,2,16,2176]{3,2,1,0:T(8,128)S(1)}, f32[4,2,16,2176]{3,2,1,0:T(8,128)S(1)}, u32[]{:S(2)}, u32[]{:S(2)}) collective-permute-start(f32[4,2,16,2176]{3,2,1,0:T(8,128)S(1)} %get-tuple-element.35), channel_id=1, source_target_pairs={{0,32},{32,0},{64,96},{96,64},{128,160},{160,128},{192,224},{224,1... | collective-permute-start | bytes 3342344 | tf_op jit(solution)/shard_map/ppermute | solution.py:374
  144.8 14.9 %all-to-all-start.6 = ((f32[4,128,256]{2,1,0:T(8,128)}), f32[4,128,256]{2,1,0:T(8,128)S(1)}, u32[]{:S(2)}, u32[]{:S(2)}) async-start(f32[4,128,256]{2,1,0:T(8,128)} %get-tuple-element.37), calls=%async_computation.6 | async-start | bytes 1048576 | tf_op jit(solution)/shard_map/all_to_all | solution.py:280
  148.3 15.8 %collective-permute-start.1 = (f32[2,16,2176]{2,1,0:T(8,128)S(1)}, f32[2,16,2176]{2,1,0:T(8,128)S(1)}, u32[]{:S(2)}, u32[]{:S(2)}) collective-permute-start(f32[2,16,2176]{2,1,0:T(8,128)S(1)} %get-tuple-element.41), channel_id=1, source_target_pairs={{0,128},{32,160},{64,192},{96,224},{128,256},{160,288},{192,320},{... | collective-permute-start | bytes 835592 | tf_op jit(solution)/shard_map/ppermute | solution.py:381
  151.6 12.6 %collective-permute-start.3 = (f32[2,16,2176]{2,1,0:T(8,128)S(1)}, f32[2,16,2176]{2,1,0:T(8,128)S(1)}, u32[]{:S(2)}, u32[]{:S(2)}) collective-permute-start(f32[2,16,2176]{2,1,0:T(8,128)S(1)} %get-tuple-element.42), channel_id=1, source_target_pairs={{0,384},{32,416},{64,448},{96,480},{128,0},{160,32},{192,64},{224,... | collective-permute-start | bytes 835592 | tf_op jit(solution)/shard_map/ppermute | solution.py:381
  154.2 11.9 %collective-permute-start.2 = (f32[2,16,2176]{2,1,0:T(8,128)S(1)}, f32[2,16,2176]{2,1,0:T(8,128)S(1)}, u32[]{:S(2)}, u32[]{:S(2)}) collective-permute-start(f32[2,16,2176]{2,1,0:T(8,128)S(1)} %get-tuple-element.43), channel_id=1, source_target_pairs={{0,256},{32,288},{64,320},{96,352},{128,384},{160,416},{192,448},{... | collective-permute-start | bytes 835592 | tf_op jit(solution)/shard_map/ppermute | solution.py:381
  160.4 15.3 %all-to-all-start.7 = ((f32[8,16,256]{2,1,0:T(8,128)}), f32[8,16,256]{2,1,0:T(8,128)S(1)}, u32[]{:S(2)}, u32[]{:S(2)}) async-start(f32[8,16,256]{2,1,0:T(8,128)} %bitcast.3), calls=%async_computation.7 | async-start | bytes 262144 | tf_op jit(solution)/shard_map/all_to_all | solution.py:280
  176.5 22.8 %all-to-all-start.8 = ((f32[8,16,256]{2,1,0:T(8,128)}), f32[8,16,256]{2,1,0:T(8,128)S(1)}, u32[]{:S(2)}, u32[]{:S(2)}) async-start(f32[8,16,256]{2,1,0:T(8,128)} %shard_map.77), calls=%async_computation.8 | async-start | bytes 262144 | tf_op jit(solution)/shard_map/all_to_all | solution.py:280
  180.7 24.0 %collective-permute-start.4 = (f32[16,2176]{1,0:T(8,128)S(1)}, f32[16,2176]{1,0:T(8,128)S(1)}, u32[]{:S(2)}, u32[]{:S(2)}) collective-permute-start(f32[16,2176]{1,0:T(8,128)S(1)} %slice_bitcast_fusion.3), channel_id=1, source_target_pairs={{0,64},{32,96},{64,0},{96,32},{128,192},{160,224},{192,128},{224,1... | collective-permute-start | bytes 417800 | tf_op jit(solution)/shard_map/ppermute | solution.py:387
  200.1 12.6 %all-to-all-start.9 = ((f32[4,128,256]{2,1,0:T(8,128)}), f32[4,128,256]{2,1,0:T(8,128)S(1)}, u32[]{:S(2)}, u32[]{:S(2)}) async-start(f32[4,128,256]{2,1,0:T(8,128)} %broadcast_in_dim.8), calls=%async_computation.9 | async-start | bytes 1048576 | tf_op jit(solution)/shard_map/all_to_all | solution.py:280

commit v6 on v5

--- a/solution.py
+++ b/solution.py
@@ -214,40 +214,48 @@
 
 
 def grad_kernel(
-    rows_ref, partition_ref, scale_ref, exp_ref, student_ref, flip_ref, back_ref,
-    weight_ref, inv_ref, keep_ref, send_ref, pull_ref, factor, softener, logits,
+    rows_ref, partition_ref, scale_ref, exp_ref, student_ref, back_ref,
+    logits_ref, pull_ref, loss_ref, factor, softener,
 ):
     total = jnp.sum(rows_ref[...], axis=0)
     partition = partition_ref[...]
     scale = 1.0 / total[0:4, :]
     losses = jnp.log(partition) - scale * total[4:8, :] * (1.0 / STUDENT_TEMP)
     loss = jnp.sum(jnp.sum(losses, axis=1, keepdims=True), axis=0, keepdims=True)
-    columns = exp_ref.shape[1]
-    for ref in (keep_ref, send_ref):
-        ref[:, :, :, columns:] = jnp.broadcast_to(loss[None, None], ref.shape[:3] + (LANES,))
+    loss_ref[...] = jnp.broadcast_to(loss, loss_ref.shape)
     softener_rows = 1.0 / partition
     for j in range(4):
         rows = slice(j * LANES, (j + 1) * LANES)
         factor[rows, :] = column(scale[j : j + 1, :])
         softener[rows, :] = column(softener_rows[j : j + 1, :])
-    width = logits.shape[1]
-    batch_index = lax.axis_index("batch")
-    core, x_index, z_high = batch_index & 1, batch_index >> 2, (batch_index >> 1) & 1
-    wide = (LANES, width)
-    for block in range(columns // width):
+    width = 512
+    for block in range(exp_ref.shape[1] // width):
         cols = slice(block * width, (block + 1) * width)
         for j in range(4):
             rows = slice(j * LANES, (j + 1) * LANES)
             soft = jnp.concatenate([softener[rows, :]] * (width // LANES), axis=1)
             hard = jnp.concatenate([factor[rows, :]] * (width // LANES), axis=1)
             targets = hard * (exp_ref[rows, cols] * scale_ref[0:1, cols])
-            logits[rows, :] = (
+            logits_ref[rows, cols] = (
                 (student_ref[rows, cols] * soft - targets) * (1.0 / STUDENT_TEMP)
             ).astype(BF16)
-        pull = jnp.dot(logits[...], back_ref[cols, :], preferred_element_type=F32)
+        pull = jnp.dot(logits_ref[:, cols], back_ref[cols, :], preferred_element_type=F32)
         pull = pull.reshape(pull_ref.shape)
         pull_ref[...] = pull if block == 0 else pull_ref[...] + pull
-        unit = jnp.dot(flip_ref[...], logits[...], preferred_element_type=F32)
+
+
+def unit_kernel(logits_ref, loss_ref, flip_ref, weight_ref, inv_ref, keep_ref, send_ref):
+    columns = weight_ref.shape[1]
+    for ref in (keep_ref, send_ref):
+        ref[:, :, :, columns:] = jnp.broadcast_to(
+            loss_ref[0:1, :][None, None], ref.shape[:3] + (LANES,)
+        )
+    batch_index = lax.axis_index("batch")
+    core, x_index, z_high = batch_index & 1, batch_index >> 2, (batch_index >> 1) & 1
+    width = 512
+    for block in range(columns // width):
+        cols = slice(block * width, (block + 1) * width)
+        unit = jnp.dot(flip_ref[...], logits_ref[:, cols], preferred_element_type=F32)
         inverse = inv_ref[:, cols]
         weight_unit = weight_ref[:, cols].astype(F32) * inverse
         inner = jnp.sum(weight_unit * unit, axis=0, keepdims=True)
@@ -362,14 +370,17 @@
     rows = exchange(rows, "head")
 
     part = shape((4, 2, share_rows, columns + LANES))
-    keep, send, pull = kernel_call(
+    grad_logits, pull, loss_part = kernel_call(
         grad_kernel,
-        (part, part, shape((4, total // 4, feature_dim))),
-        [tail, tail, pltpu.VMEM((total, 512), BF16)],
-        limit=16,
-    )(
-        rows, partition, col_scale, teacher_exp, student_exp, flip, back, weight,
-        weight_inv,
+        (
+            shape((total, columns), BF16),
+            shape((4, total // 4, feature_dim)),
+            shape((8, LANES)),
+        ),
+        [tail, tail],
+    )(rows, partition, col_scale, teacher_exp, student_exp, back)
+    keep, send = kernel_call(unit_kernel, (part, part))(
+        grad_logits, loss_part, flip, weight, weight_inv
     )
     parts = keep + lax.ppermute(send, "batch", [(i, i ^ 1) for i in range(16)])
     parts, pull = tie(parts, pull)

time: 215 us -> 216 us (level)
    pallas_call x11 -> x12, Pallas kernels: 11.6 us -> 11.9 us  [call(): pl.pallas_call(body, out_shape=out_shape, in_specs=specs, out_specs=jax.t...]
where the time goes in v6:
time: 216 us; the launch traced here: 215 us
  blocking collectives  129 us (60%)
  waiting for transfers between devices  36.8 us (17%)
  starting transfers between devices  31.5 us (15%)
  Pallas kernels  11.9 us (6%)
  local copies, waits for them, and re-layouts  2.87 us (1%)
  between operations  2.57 us (1%)
    all_to_all x6, blocking collectives, exchange(): return lax.all_to_all(blocks, axis, 0, 0, axis_index_groups=groups)  123 us
    all_to_all x4, waiting for transfers between devices, exchange(): return lax.all_to_all(blocks, axis, 0, 0, axis_index_groups=groups)  32.2 us
    all_to_all x4, starting transfers between devices, exchange(): return lax.all_to_all(blocks, axis, 0, 0, axis_index_groups=groups)  15.9 us
    pallas_call x12, Pallas kernels, call(): pl.pallas_call(body, out_shape=out_shape, in_specs=specs, out_specs=jax.t...  11.9 us
    ppermute x3, starting transfers between devices, per_device(): held = held + lax.ppermute(parts[step], 'batch', pairs)  11.3 us
    all_gather x3, blocking collectives, over_batch(): both = lax.all_gather(block, 'batch', axis_index_groups=pairs)  5.44 us
  transfers between devices with their start and end apart: 9, of which 5 were waited for; matrix products, arithmetic and copies ran while one was open for 1% of the time, Pallas kernels for 0%

profile of v6, /device:TPU:4, one launch (start us, length us, event | category | flops | bytes accessed | tf_op | source)
XLA Modules:
  0.0 215.0 jit_solution(8382510633637165518)
XLA Ops:
  0.6 4.6 %shard_map.67 = (bf16[2048,256]{1,0:T(8,128)(2,1)S(1)}, f32[1,2048]{1,0:T(1,128)S(1)}, f32[512,2048]{1,0:T(8,128)S(1)}, f32[16,128]{1,0:T(8,128)S(1)}, f32[16,25...) custom-call(bf16[256,2048]{1,0:T(8,128)(2,1)} %weight_ref.1, ...), custom_call_target="tpu_custom_call" | custom-call | tf_op jit(solution)/shard_map/pallas_call | solution.py:27
  5.2 1.8 all-gather
  7.0 30.6 %all_to_all.50.refs_0_ = f32[8,16,128]{2,1,0:T(8,128)S(1)} all-to-all(f32[8,16,128]{2,1,0:T(8,128)S(1)} %shard_map.68), channel_id=1, replica_groups={{0,64,128,192,256,320,384,448},{32,96,160,224,288,352,416,480},{1,65,12..., dimensions={0} | all-to-all | bytes 131072 | tf_op jit(solution)/shard_map/all_to_all | solution.py:288
  38.3 21.4 %all_to_all.51.rows_ref = f32[32,8,128]{2,1,0:T(8,128)S(1)} all-to-all(f32[32,8,128]{2,1,0:T(8,128)S(1)} %shard_map.69), channel_id=1, replica_groups=mesh['batch'=16,'head'=32] {'head'}, dimensions={0} | all-to-all | bytes 262144 | tf_op jit(solution)/shard_map/all_to_all | solution.py:288
  60.2 1.8 all-gather.1
  62.1 17.5 %all_to_all.52.refs_0_ = f32[8,16,128]{2,1,0:T(8,128)S(1)} all-to-all(f32[8,16,128]{2,1,0:T(8,128)S(1)} %shard_map.71), channel_id=1, replica_groups={{0,64,128,192,256,320,384,448},{32,96,160,224,288,352,416,480},{1,65,12..., dimensions={0} | all-to-all | bytes 131072 | tf_op jit(solution)/shard_map/all_to_all | solution.py:288
  80.2 17.6 %all_to_all.53.rows_ref = f32[32,4,128]{2,1,0:T(4,128)S(1)} all-to-all(f32[32,4,128]{2,1,0:T(4,128)S(1)} %shard_map.72), channel_id=1, replica_groups=mesh['batch'=16,'head'=32] {'head'}, dimensions={0} | all-to-all | bytes 131072 | tf_op jit(solution)/shard_map/all_to_all | solution.py:288
  98.3 1.8 all-gather.2
  100.1 17.5 %all_to_all.54.cols_ref = f32[8,16,128]{2,1,0:T(8,128)S(1)} all-to-all(f32[8,16,128]{2,1,0:T(8,128)S(1)} %shard_map.74), channel_id=1, replica_groups={{0,64,128,192,256,320,384,448},{32,96,160,224,288,352,416,480},{1,65,12..., dimensions={0} | all-to-all | bytes 131072 | tf_op jit(solution)/shard_map/all_to_all | solution.py:288
  117.6 1.2 shard_map.75
  118.8 18.5 %all_to_all.55.rows_ref = f32[32,8,128]{2,1,0:T(8,128)S(1)} all-to-all(f32[32,8,128]{2,1,0:T(8,128)S(1)} %get-tuple-element.29), channel_id=1, replica_groups=mesh['batch'=16,'head'=32] {'head'}, dimensions={0} | all-to-all | bytes 262144 | tf_op jit(solution)/shard_map/all_to_all | solution.py:288
  137.3 2.0 shard_map.76
  139.3 1.1 shard_map.77
  140.4 1.9 collective-permute-start
  142.3 2.7 %collective-permute-done = f32[4,2,16,2176]{3,2,1,0:T(8,128)S(1)} collective-permute-done((f32[4,2,16,2176]{3,2,1,0:T(8,128)S(1)}, f32[4,2,16,2176]{3,2,1,0:T(8,128)S(1)}, u32[]{:S(2)}, u32[]{:S(2)}) %collective-permute-start) | collective-permute-done | bytes 1114144 | tf_op jit(solution)/shard_map/ppermute | solution.py:385
  145.1 3.5 %all-to-all-start.6 = ((f32[4,128,256]{2,1,0:T(8,128)}), f32[4,128,256]{2,1,0:T(8,128)S(1)}, u32[]{:S(2)}, u32[]{:S(2)}) async-start(f32[4,128,256]{2,1,0:T(8,128)} %get-tuple-element.41), calls=%async_computation.6 | async-start | bytes 1048576 | tf_op jit(solution)/shard_map/all_to_all | solution.py:288
  148.7 3.2 %collective-permute-start.1 = (f32[2,16,2176]{2,1,0:T(8,128)S(1)}, f32[2,16,2176]{2,1,0:T(8,128)S(1)}, u32[]{:S(2)}, u32[]{:S(2)}) collective-permute-start(f32[2,16,2176]{2,1,0:T(8,128)S(1)} %get-tuple-element.45), channel_id=1, source_target_pairs={{0,128},{32,160},{64,192},{96,224},{128,256},{160,288},{192,320},{... | collective-permute-start | bytes 835592 | tf_op jit(solution)/shard_map/ppermute | solution.py:392
  151.9 2.6 %collective-permute-start.3 = (f32[2,16,2176]{2,1,0:T(8,128)S(1)}, f32[2,16,2176]{2,1,0:T(8,128)S(1)}, u32[]{:S(2)}, u32[]{:S(2)}) collective-permute-start(f32[2,16,2176]{2,1,0:T(8,128)S(1)} %get-tuple-element.46), channel_id=1, source_target_pairs={{0,384},{32,416},{64,448},{96,480},{128,0},{160,32},{192,64},{224,... | collective-permute-start | bytes 835592 | tf_op jit(solution)/shard_map/ppermute | solution.py:392
  154.6 5.5 %collective-permute-start.2 = (f32[2,16,2176]{2,1,0:T(8,128)S(1)}, f32[2,16,2176]{2,1,0:T(8,128)S(1)}, u32[]{:S(2)}, u32[]{:S(2)}) collective-permute-start(f32[2,16,2176]{2,1,0:T(8,128)S(1)} %get-tuple-element.47), channel_id=1, source_target_pairs={{0,256},{32,288},{64,320},{96,352},{128,384},{160,416},{192,448},{... | collective-permute-start | bytes 835592 | tf_op jit(solution)/shard_map/ppermute | solution.py:392
  160.0 0.7 reduce_sum.9
  160.7 3.8 %all-to-all-start.7 = ((f32[8,16,256]{2,1,0:T(8,128)}), f32[8,16,256]{2,1,0:T(8,128)S(1)}, u32[]{:S(2)}, u32[]{:S(2)}) async-start(f32[8,16,256]{2,1,0:T(8,128)} %bitcast.3), calls=%async_computation.7 | async-start | bytes 262144 | tf_op jit(solution)/shard_map/all_to_all | solution.py:288
  164.5 1.9 collective-permute-done.2
  166.5 9.6 %all-to-all-done.7.blocks_ref = f32[8,16,256]{2,1,0:T(8,128)S(1)} async-done(((f32[8,16,256]{2,1,0:T(8,128)}), f32[8,16,256]{2,1,0:T(8,128)S(1)}, u32[]{:S(2)}, u32[]{:S(2)}) %all-to-all-start.7) | async-done | bytes 131104 | tf_op jit(solution)/shard_map/all_to_all | solution.py:288
  176.1 0.8 shard_map.78
  176.8 4.2 %all-to-all-start.8 = ((f32[8,16,256]{2,1,0:T(8,128)}), f32[8,16,256]{2,1,0:T(8,128)S(1)}, u32[]{:S(2)}, u32[]{:S(2)}) async-start(f32[8,16,256]{2,1,0:T(8,128)} %shard_map.78), calls=%async_computation.8 | async-start | bytes 262144 | tf_op jit(solution)/shard_map/all_to_all | solution.py:288
  181.0 2.3 %collective-permute-start.4 = (f32[16,2176]{1,0:T(8,128)S(1)}, f32[16,2176]{1,0:T(8,128)S(1)}, u32[]{:S(2)}, u32[]{:S(2)}) collective-permute-start(f32[16,2176]{1,0:T(8,128)S(1)} %slice_bitcast_fusion.3), channel_id=1, source_target_pairs={{0,64},{32,96},{64,0},{96,32},{128,192},{160,224},{192,128},{224,1... | collective-permute-start | bytes 417800 | tf_op jit(solution)/shard_map/ppermute | solution.py:398
  183.3 16.3 %all-to-all-done.8 = f32[8,16,256]{2,1,0:T(8,128)S(1)} async-done(((f32[8,16,256]{2,1,0:T(8,128)}), f32[8,16,256]{2,1,0:T(8,128)S(1)}, u32[]{:S(2)}, u32[]{:S(2)}) %all-to-all-start.8) | async-done | bytes 131104 | tf_op jit(solution)/shard_map/all_to_all | solution.py:288
  199.6 0.8 broadcast_in_dim.8
  200.5 4.5 %all-to-all-start.9 = ((f32[4,128,256]{2,1,0:T(8,128)}), f32[4,128,256]{2,1,0:T(8,128)S(1)}, u32[]{:S(2)}, u32[]{:S(2)}) async-start(f32[4,128,256]{2,1,0:T(8,128)} %broadcast_in_dim.8), calls=%async_computation.9 | async-start | bytes 1048576 | tf_op jit(solution)/shard_map/all_to_all | solution.py:288
  205.5 0.7 slice.34
  206.8 6.2 %all-to-all-done.9 = f32[4,128,256]{2,1,0:T(8,128)S(1)} async-done(((f32[4,128,256]{2,1,0:T(8,128)}), f32[4,128,256]{2,1,0:T(8,128)S(1)}, u32[]{:S(2)}, u32[]{:S(2)}) %all-to-all-start.9) | async-done | bytes 524320 | tf_op jit(solution)/shard_map/all_to_all | solution.py:288
  213.0 0.8 copy.8
  (19 shorter events, 3.1 us)
Async XLA Ops:
  137.3 2.0 copy-start
  140.4 4.6 %collective-permute-start = (f32[4,2,16,2176]{3,2,1,0:T(8,128)S(1)}, f32[4,2,16,2176]{3,2,1,0:T(8,128)S(1)}, u32[]{:S(2)}, u32[]{:S(2)}) collective-permute-start(f32[4,2,16,2176]{3,2,1,0:T(8,128)S(1)} %get-tuple-element.39), channel_id=1, source_target_pairs={{0,32},{32,0},{64,96},{96,64},{128,160},{160,128},{192,224},{224,1... | collective-permute-start | bytes 3342344 | tf_op jit(solution)/shard_map/ppermute | solution.py:385
  145.1 14.9 %all-to-all-start.6 = ((f32[4,128,256]{2,1,0:T(8,128)}), f32[4,128,256]{2,1,0:T(8,128)S(1)}, u32[]{:S(2)}, u32[]{:S(2)}) async-start(f32[4,128,256]{2,1,0:T(8,128)} %get-tuple-element.41), calls=%async_computation.6 | async-start | bytes 1048576 | tf_op jit(solution)/shard_map/all_to_all | solution.py:288
  148.7 15.8 %collective-permute-start.1 = (f32[2,16,2176]{2,1,0:T(8,128)S(1)}, f32[2,16,2176]{2,1,0:T(8,128)S(1)}, u32[]{:S(2)}, u32[]{:S(2)}) collective-permute-start(f32[2,16,2176]{2,1,0:T(8,128)S(1)} %get-tuple-element.45), channel_id=1, source_target_pairs={{0,128},{32,160},{64,192},{96,224},{128,256},{160,288},{192,320},{... | collective-permute-start | bytes 835592 | tf_op jit(solution)/shard_map/ppermute | solution.py:392
  151.9 12.6 %collective-permute-start.3 = (f32[2,16,2176]{2,1,0:T(8,128)S(1)}, f32[2,16,2176]{2,1,0:T(8,128)S(1)}, u32[]{:S(2)}, u32[]{:S(2)}) collective-permute-start(f32[2,16,2176]{2,1,0:T(8,128)S(1)} %get-tuple-element.46), channel_id=1, source_target_pairs={{0,384},{32,416},{64,448},{96,480},{128,0},{160,32},{192,64},{224,... | collective-permute-start | bytes 835592 | tf_op jit(solution)/shard_map/ppermute | solution.py:392
  154.6 11.9 %collective-permute-start.2 = (f32[2,16,2176]{2,1,0:T(8,128)S(1)}, f32[2,16,2176]{2,1,0:T(8,128)S(1)}, u32[]{:S(2)}, u32[]{:S(2)}) collective-permute-start(f32[2,16,2176]{2,1,0:T(8,128)S(1)} %get-tuple-element.47), channel_id=1, source_target_pairs={{0,256},{32,288},{64,320},{96,352},{128,384},{160,416},{192,448},{... | collective-permute-start | bytes 835592 | tf_op jit(solution)/shard_map/ppermute | solution.py:392
  160.7 15.3 %all-to-all-start.7 = ((f32[8,16,256]{2,1,0:T(8,128)}), f32[8,16,256]{2,1,0:T(8,128)S(1)}, u32[]{:S(2)}, u32[]{:S(2)}) async-start(f32[8,16,256]{2,1,0:T(8,128)} %bitcast.3), calls=%async_computation.7 | async-start | bytes 262144 | tf_op jit(solution)/shard_map/all_to_all | solution.py:288
  176.8 22.8 %all-to-all-start.8 = ((f32[8,16,256]{2,1,0:T(8,128)}), f32[8,16,256]{2,1,0:T(8,128)S(1)}, u32[]{:S(2)}, u32[]{:S(2)}) async-start(f32[8,16,256]{2,1,0:T(8,128)} %shard_map.78), calls=%async_computation.8 | async-start | bytes 262144 | tf_op jit(solution)/shard_map/all_to_all | solution.py:288
  181.0 24.0 %collective-permute-start.4 = (f32[16,2176]{1,0:T(8,128)S(1)}, f32[16,2176]{1,0:T(8,128)S(1)}, u32[]{:S(2)}, u32[]{:S(2)}) collective-permute-start(f32[16,2176]{1,0:T(8,128)S(1)} %slice_bitcast_fusion.3), channel_id=1, source_target_pairs={{0,64},{32,96},{64,0},{96,32},{128,192},{160,224},{192,128},{224,1... | collective-permute-start | bytes 417800 | tf_op jit(solution)/shard_map/ppermute | solution.py:398
  200.5 12.6 %all-to-all-start.9 = ((f32[4,128,256]{2,1,0:T(8,128)}), f32[4,128,256]{2,1,0:T(8,128)S(1)}, u32[]{:S(2)}, u32[]{:S(2)}) async-start(f32[4,128,256]{2,1,0:T(8,128)} %broadcast_in_dim.8), calls=%async_computation.9 | async-start | bytes 1048576 | tf_op jit(solution)/shard_map/all_to_all | solution.py:288

commit v7 on v5

--- a/solution.py
+++ b/solution.py
@@ -365,7 +365,7 @@
     keep, send, pull = kernel_call(
         grad_kernel,
         (part, part, shape((4, total // 4, feature_dim))),
-        [tail, tail, pltpu.VMEM((total, 512), BF16)],
+        [tail, tail, pltpu.VMEM((total, 1024), BF16)],
         limit=16,
     )(
         rows, partition, col_scale, teacher_exp, student_exp, flip, back, weight,

time: 215 us -> 215 us (level)
  no operation moved by 1% of the time
where the time goes in v7:
time: 215 us
  blocking collectives  129 us (60%)
  waiting for transfers between devices  36.8 us (17%)
  starting transfers between devices  31.4 us (15%)
  Pallas kernels  11.6 us (5%)
  local copies, waits for them, and re-layouts  2.87 us (1%)
  between operations  2.56 us (1%)
    all_to_all x6, blocking collectives, exchange(): return lax.all_to_all(blocks, axis, 0, 0, axis_index_groups=groups)  123 us
    all_to_all x4, waiting for transfers between devices, exchange(): return lax.all_to_all(blocks, axis, 0, 0, axis_index_groups=groups)  32.2 us
    all_to_all x4, starting transfers between devices, exchange(): return lax.all_to_all(blocks, axis, 0, 0, axis_index_groups=groups)  15.9 us
    pallas_call x11, Pallas kernels, call(): pl.pallas_call(body, out_shape=out_shape, in_specs=specs, out_specs=jax.t...  11.6 us
    ppermute x3, starting transfers between devices, per_device(): held = held + lax.ppermute(parts[step], 'batch', pairs)  11.3 us
    all_gather x3, blocking collectives, over_batch(): both = lax.all_gather(block, 'batch', axis_index_groups=pairs)  5.44 us
  transfers between devices with their start and end apart: 9, of which 5 were waited for; matrix products, arithmetic and copies ran while one was open for 1% of the time, Pallas kernels for 0%

profile of v7, /device:TPU:4, one launch (start us, length us, event | category | flops | bytes accessed | tf_op | source)
XLA Modules:
  0.0 214.6 jit_solution(10664022568854306626)
XLA Ops:
  0.6 4.6 %shard_map.67 = (bf16[2048,256]{1,0:T(8,128)(2,1)S(1)}, f32[1,2048]{1,0:T(1,128)S(1)}, f32[512,2048]{1,0:T(8,128)S(1)}, f32[16,128]{1,0:T(8,128)S(1)}, f32[16,25...) custom-call(bf16[256,2048]{1,0:T(8,128)(2,1)} %weight_ref.1, ...), custom_call_target="tpu_custom_call" | custom-call | tf_op jit(solution)/shard_map/pallas_call | solution.py:27
  5.2 1.8 all-gather
  7.0 30.6 %all_to_all.50.refs_0_ = f32[8,16,128]{2,1,0:T(8,128)S(1)} all-to-all(f32[8,16,128]{2,1,0:T(8,128)S(1)} %shard_map.68), channel_id=1, replica_groups={{0,64,128,192,256,320,384,448},{32,96,160,224,288,352,416,480},{1,65,12..., dimensions={0} | all-to-all | bytes 131072 | tf_op jit(solution)/shard_map/all_to_all | solution.py:280
  37.7 0.6 shard_map.69
  38.3 21.4 %all_to_all.51.rows_ref = f32[32,8,128]{2,1,0:T(8,128)S(1)} all-to-all(f32[32,8,128]{2,1,0:T(8,128)S(1)} %shard_map.69), channel_id=1, replica_groups=mesh['batch'=16,'head'=32] {'head'}, dimensions={0} | all-to-all | bytes 262144 | tf_op jit(solution)/shard_map/all_to_all | solution.py:280
  60.2 1.8 all-gather.1
  62.1 17.5 %all_to_all.52.refs_0_ = f32[8,16,128]{2,1,0:T(8,128)S(1)} all-to-all(f32[8,16,128]{2,1,0:T(8,128)S(1)} %shard_map.71), channel_id=1, replica_groups={{0,64,128,192,256,320,384,448},{32,96,160,224,288,352,416,480},{1,65,12..., dimensions={0} | all-to-all | bytes 131072 | tf_op jit(solution)/shard_map/all_to_all | solution.py:280
  80.2 17.6 %all_to_all.53.rows_ref = f32[32,4,128]{2,1,0:T(4,128)S(1)} all-to-all(f32[32,4,128]{2,1,0:T(4,128)S(1)} %shard_map.72), channel_id=1, replica_groups=mesh['batch'=16,'head'=32] {'head'}, dimensions={0} | all-to-all | bytes 131072 | tf_op jit(solution)/shard_map/all_to_all | solution.py:280
  98.3 1.8 all-gather.2
  100.1 17.5 %all_to_all.54.cols_ref = f32[8,16,128]{2,1,0:T(8,128)S(1)} all-to-all(f32[8,16,128]{2,1,0:T(8,128)S(1)} %shard_map.74), channel_id=1, replica_groups={{0,64,128,192,256,320,384,448},{32,96,160,224,288,352,416,480},{1,65,12..., dimensions={0} | all-to-all | bytes 131072 | tf_op jit(solution)/shard_map/all_to_all | solution.py:280
  117.6 1.2 shard_map.75
  118.8 18.5 %all_to_all.55.rows_ref = f32[32,8,128]{2,1,0:T(8,128)S(1)} all-to-all(f32[32,8,128]{2,1,0:T(8,128)S(1)} %get-tuple-element.27), channel_id=1, replica_groups=mesh['batch'=16,'head'=32] {'head'}, dimensions={0} | all-to-all | bytes 262144 | tf_op jit(solution)/shard_map/all_to_all | solution.py:280
  137.3 2.7 %shard_map.76 = (f32[4,2,16,2176]{3,2,1,0:T(8,128)S(1)}, f32[4,2,16,2176]{3,2,1,0:T(8,128)S(1)}, f32[4,128,256]{2,1,0:T(8,128)}) custom-call(f32[32,8,128]{2,1,0:T(8,128)S(1)} %all_to_all.55.rows_ref, f32[4,128]{1,0:T(4,128)S(1)} %get-tuple-element.28.partition_ref, f32[8,2048]{1,0:T(8,128)S(1)} %get-tuple-element.29.scale_ref, ...), custom_call_target="tpu_custom_call" | custom-call | tf_op jit(solution)/shard_map/pallas_call | solution.py:27
  140.0 1.9 collective-permute-start
  142.0 2.7 %collective-permute-done = f32[4,2,16,2176]{3,2,1,0:T(8,128)S(1)} collective-permute-done((f32[4,2,16,2176]{3,2,1,0:T(8,128)S(1)}, f32[4,2,16,2176]{3,2,1,0:T(8,128)S(1)}, u32[]{:S(2)}, u32[]{:S(2)}) %collective-permute-start) | collective-permute-done | bytes 1114144 | tf_op jit(solution)/shard_map/ppermute | solution.py:374
  144.8 3.5 %all-to-all-start.6 = ((f32[4,128,256]{2,1,0:T(8,128)}), f32[4,128,256]{2,1,0:T(8,128)S(1)}, u32[]{:S(2)}, u32[]{:S(2)}) async-start(f32[4,128,256]{2,1,0:T(8,128)} %get-tuple-element.37), calls=%async_computation.6 | async-start | bytes 1048576 | tf_op jit(solution)/shard_map/all_to_all | solution.py:280
  148.3 3.2 %collective-permute-start.1 = (f32[2,16,2176]{2,1,0:T(8,128)S(1)}, f32[2,16,2176]{2,1,0:T(8,128)S(1)}, u32[]{:S(2)}, u32[]{:S(2)}) collective-permute-start(f32[2,16,2176]{2,1,0:T(8,128)S(1)} %get-tuple-element.41), channel_id=1, source_target_pairs={{0,128},{32,160},{64,192},{96,224},{128,256},{160,288},{192,320},{... | collective-permute-start | bytes 835592 | tf_op jit(solution)/shard_map/ppermute | solution.py:381
  151.6 2.6 %collective-permute-start.3 = (f32[2,16,2176]{2,1,0:T(8,128)S(1)}, f32[2,16,2176]{2,1,0:T(8,128)S(1)}, u32[]{:S(2)}, u32[]{:S(2)}) collective-permute-start(f32[2,16,2176]{2,1,0:T(8,128)S(1)} %get-tuple-element.42), channel_id=1, source_target_pairs={{0,384},{32,416},{64,448},{96,480},{128,0},{160,32},{192,64},{224,... | collective-permute-start | bytes 835592 | tf_op jit(solution)/shard_map/ppermute | solution.py:381
  154.2 5.5 %collective-permute-start.2 = (f32[2,16,2176]{2,1,0:T(8,128)S(1)}, f32[2,16,2176]{2,1,0:T(8,128)S(1)}, u32[]{:S(2)}, u32[]{:S(2)}) collective-permute-start(f32[2,16,2176]{2,1,0:T(8,128)S(1)} %get-tuple-element.43), channel_id=1, source_target_pairs={{0,256},{32,288},{64,320},{96,352},{128,384},{160,416},{192,448},{... | collective-permute-start | bytes 835592 | tf_op jit(solution)/shard_map/ppermute | solution.py:381
  159.7 0.7 reduce_sum.9
  160.4 3.8 %all-to-all-start.7 = ((f32[8,16,256]{2,1,0:T(8,128)}), f32[8,16,256]{2,1,0:T(8,128)S(1)}, u32[]{:S(2)}, u32[]{:S(2)}) async-start(f32[8,16,256]{2,1,0:T(8,128)} %bitcast.3), calls=%async_computation.7 | async-start | bytes 262144 | tf_op jit(solution)/shard_map/all_to_all | solution.py:280
  164.2 1.9 collective-permute-done.2
  166.1 9.6 %all-to-all-done.7.blocks_ref = f32[8,16,256]{2,1,0:T(8,128)S(1)} async-done(((f32[8,16,256]{2,1,0:T(8,128)}), f32[8,16,256]{2,1,0:T(8,128)S(1)}, u32[]{:S(2)}, u32[]{:S(2)}) %all-to-all-start.7) | async-done | bytes 131104 | tf_op jit(solution)/shard_map/all_to_all | solution.py:280
  175.7 0.8 shard_map.77
  176.5 4.2 %all-to-all-start.8 = ((f32[8,16,256]{2,1,0:T(8,128)}), f32[8,16,256]{2,1,0:T(8,128)S(1)}, u32[]{:S(2)}, u32[]{:S(2)}) async-start(f32[8,16,256]{2,1,0:T(8,128)} %shard_map.77), calls=%async_computation.8 | async-start | bytes 262144 | tf_op jit(solution)/shard_map/all_to_all | solution.py:280
  180.7 2.3 %collective-permute-start.4 = (f32[16,2176]{1,0:T(8,128)S(1)}, f32[16,2176]{1,0:T(8,128)S(1)}, u32[]{:S(2)}, u32[]{:S(2)}) collective-permute-start(f32[16,2176]{1,0:T(8,128)S(1)} %slice_bitcast_fusion.3), channel_id=1, source_target_pairs={{0,64},{32,96},{64,0},{96,32},{128,192},{160,224},{192,128},{224,1... | collective-permute-start | bytes 417800 | tf_op jit(solution)/shard_map/ppermute | solution.py:387
  182.9 16.3 %all-to-all-done.8 = f32[8,16,256]{2,1,0:T(8,128)S(1)} async-done(((f32[8,16,256]{2,1,0:T(8,128)}), f32[8,16,256]{2,1,0:T(8,128)S(1)}, u32[]{:S(2)}, u32[]{:S(2)}) %all-to-all-start.8) | async-done | bytes 131104 | tf_op jit(solution)/shard_map/all_to_all | solution.py:280
  199.3 0.8 broadcast_in_dim.8
  200.1 4.5 %all-to-all-start.9 = ((f32[4,128,256]{2,1,0:T(8,128)}), f32[4,128,256]{2,1,0:T(8,128)S(1)}, u32[]{:S(2)}, u32[]{:S(2)}) async-start(f32[4,128,256]{2,1,0:T(8,128)} %broadcast_in_dim.8), calls=%async_computation.9 | async-start | bytes 1048576 | tf_op jit(solution)/shard_map/all_to_all | solution.py:280
  205.1 0.7 slice.34
  206.5 6.2 %all-to-all-done.9 = f32[4,128,256]{2,1,0:T(8,128)S(1)} async-done(((f32[4,128,256]{2,1,0:T(8,128)}), f32[4,128,256]{2,1,0:T(8,128)S(1)}, u32[]{:S(2)}, u32[]{:S(2)}) %all-to-all-start.9) | async-done | bytes 524320 | tf_op jit(solution)/shard_map/all_to_all | solution.py:280
  212.7 0.8 copy.8
  (18 shorter events, 2.5 us)
Async XLA Ops:
  117.6 19.7 %copy-start = (bf16[256,2048]{1,0:T(8,128)(2,1)S(1)}, bf16[256,2048]{1,0:T(8,128)(2,1)}, u32[]{:S(2)}) copy-start(bf16[256,2048]{1,0:T(8,128)(2,1)} %weight_ref.1) | copy-start | bytes 3145732
  140.0 4.6 %collective-permute-start = (f32[4,2,16,2176]{3,2,1,0:T(8,128)S(1)}, f32[4,2,16,2176]{3,2,1,0:T(8,128)S(1)}, u32[]{:S(2)}, u32[]{:S(2)}) collective-permute-start(f32[4,2,16,2176]{3,2,1,0:T(8,128)S(1)} %get-tuple-element.35), channel_id=1, source_target_pairs={{0,32},{32,0},{64,96},{96,64},{128,160},{160,128},{192,224},{224,1... | collective-permute-start | bytes 3342344 | tf_op jit(solution)/shard_map/ppermute | solution.py:374
  144.8 14.9 %all-to-all-start.6 = ((f32[4,128,256]{2,1,0:T(8,128)}), f32[4,128,256]{2,1,0:T(8,128)S(1)}, u32[]{:S(2)}, u32[]{:S(2)}) async-start(f32[4,128,256]{2,1,0:T(8,128)} %get-tuple-element.37), calls=%async_computation.6 | async-start | bytes 1048576 | tf_op jit(solution)/shard_map/all_to_all | solution.py:280
  148.3 15.8 %collective-permute-start.1 = (f32[2,16,2176]{2,1,0:T(8,128)S(1)}, f32[2,16,2176]{2,1,0:T(8,128)S(1)}, u32[]{:S(2)}, u32[]{:S(2)}) collective-permute-start(f32[2,16,2176]{2,1,0:T(8,128)S(1)} %get-tuple-element.41), channel_id=1, source_target_pairs={{0,128},{32,160},{64,192},{96,224},{128,256},{160,288},{192,320},{... | collective-permute-start | bytes 835592 | tf_op jit(solution)/shard_map/ppermute | solution.py:381
  151.6 12.6 %collective-permute-start.3 = (f32[2,16,2176]{2,1,0:T(8,128)S(1)}, f32[2,16,2176]{2,1,0:T(8,128)S(1)}, u32[]{:S(2)}, u32[]{:S(2)}) collective-permute-start(f32[2,16,2176]{2,1,0:T(8,128)S(1)} %get-tuple-element.42), channel_id=1, source_target_pairs={{0,384},{32,416},{64,448},{96,480},{128,0},{160,32},{192,64},{224,... | collective-permute-start | bytes 835592 | tf_op jit(solution)/shard_map/ppermute | solution.py:381
  154.2 11.9 %collective-permute-start.2 = (f32[2,16,2176]{2,1,0:T(8,128)S(1)}, f32[2,16,2176]{2,1,0:T(8,128)S(1)}, u32[]{:S(2)}, u32[]{:S(2)}) collective-permute-start(f32[2,16,2176]{2,1,0:T(8,128)S(1)} %get-tuple-element.43), channel_id=1, source_target_pairs={{0,256},{32,288},{64,320},{96,352},{128,384},{160,416},{192,448},{... | collective-permute-start | bytes 835592 | tf_op jit(solution)/shard_map/ppermute | solution.py:381
  160.4 15.3 %all-to-all-start.7 = ((f32[8,16,256]{2,1,0:T(8,128)}), f32[8,16,256]{2,1,0:T(8,128)S(1)}, u32[]{:S(2)}, u32[]{:S(2)}) async-start(f32[8,16,256]{2,1,0:T(8,128)} %bitcast.3), calls=%async_computation.7 | async-start | bytes 262144 | tf_op jit(solution)/shard_map/all_to_all | solution.py:280
  176.5 22.8 %all-to-all-start.8 = ((f32[8,16,256]{2,1,0:T(8,128)}), f32[8,16,256]{2,1,0:T(8,128)S(1)}, u32[]{:S(2)}, u32[]{:S(2)}) async-start(f32[8,16,256]{2,1,0:T(8,128)} %shard_map.77), calls=%async_computation.8 | async-start | bytes 262144 | tf_op jit(solution)/shard_map/all_to_all | solution.py:280
  180.7 24.0 %collective-permute-start.4 = (f32[16,2176]{1,0:T(8,128)S(1)}, f32[16,2176]{1,0:T(8,128)S(1)}, u32[]{:S(2)}, u32[]{:S(2)}) collective-permute-start(f32[16,2176]{1,0:T(8,128)S(1)} %slice_bitcast_fusion.3), channel_id=1, source_target_pairs={{0,64},{32,96},{64,0},{96,32},{128,192},{160,224},{192,128},{224,1... | collective-permute-start | bytes 417800 | tf_op jit(solution)/shard_map/ppermute | solution.py:387
  200.1 12.6 %all-to-all-start.9 = ((f32[4,128,256]{2,1,0:T(8,128)}), f32[4,128,256]{2,1,0:T(8,128)S(1)}, u32[]{:S(2)}, u32[]{:S(2)}) async-start(f32[4,128,256]{2,1,0:T(8,128)} %broadcast_in_dim.8), calls=%async_computation.9 | async-start | bytes 1048576 | tf_op jit(solution)/shard_map/all_to_all | solution.py:280
